TPU v7x, 32 devices: a whole 2x2x4 slice. The times are simulated.
32 devices in a mesh: dp: 4 (over y, x), fsdp: 8 (over z, core).
Axes of the slice: x: 2, y: 2, z: 4, core: 2. Of those that a mesh axis runs over, the one named last changes fastest.
Arguments:
- tokens: bfloat16 [2, 32, 1024, 1024], P(None, ('dp', 'fsdp')), may hold values from -6 to 6
- document_length_list: int32 [2, 32, 8], P(None, ('dp', 'fsdp')), may hold values from 1 to 256, 1024 in all within a row
- joint_projection_weight: bfloat16 [1024, 3072], P('fsdp'), may hold values from -0.25 to 0.25
- attention_out_weight: bfloat16 [1024, 1024], P('fsdp'), may hold values from -0.375 to 0.375
- feed_up_weight: bfloat16 [1024, 4096], P('fsdp'), may hold values from -0.1875 to 0.1875
- feed_down_weight: bfloat16 [4096, 1024], P('fsdp'), may hold values from -0.09375 to 0.09375
- frozen_norm_gains: bfloat16 [2, 1024], P(None, 'fsdp'), may hold values from 0.5 to 1.5
- biases: bfloat16 [6, 1024], P(None, 'fsdp'), may hold values from -4 to 4
- hidden_up_bias: bfloat16 [4096], P('fsdp'), may hold values from -6 to 6
- query_down_adapter: bfloat16 [1024, 4], replicated, may hold values from -0.1875 to 0.1875
- query_up_adapter: bfloat16 [4, 1024], replicated, may hold values from -0.4375 to 0.4375
- value_down_adapter: bfloat16 [1024, 4], replicated, may hold values from -0.1875 to 0.1875
- value_up_adapter: bfloat16 [4, 1024], replicated, may hold values from -0.4375 to 0.4375
- cotangent: bfloat16 [2, 32, 1024, 1024], P(None, ('dp', 'fsdp')), may hold values from -6 to 6
Outputs:
- block_output: bfloat16 [2, 32, 1024, 1024], P(None, ('dp', 'fsdp'))
- input_grad: bfloat16 [2, 32, 1024, 1024], P(None, ('dp', 'fsdp'))
- grad_lora_a_q: float32 [1024, 4], replicated
- grad_lora_b_q: float32 [4, 1024], replicated
- grad_lora_a_v: float32 [1024, 4], replicated
- grad_lora_b_v: float32 [4, 1024], replicated
Inputs may be any that keep to these rules, and one draw needn't show every extreme that they name: `document_length_list`: the 8 lengths of a slot sum to 1024, and the largest of them is exactly 256.
All inputs are finite; a program needn't handle non-finite values.
Results may differ from a plain program's by a relative error of at most 0.015.
Values may be sent and summed in bfloat16 or wider, within the bound.
No kernel may reach another device: no remote copies, remote signals or barrier semaphores. Data moves between devices by JAX's collectives and lax.ppermute only.
A program may use at most 320 MiB of HBM per device.

v0:
```python
import jax
import jax.numpy as jnp
from jax import lax
from jax.sharding import PartitionSpec as P

HEADS = 16
HEAD_DIM = 64


epsilon = 1e-05
adapter_scale = 8.0
masked_fill = -1e30


def layer_norm(inputs, norm_gain, norm_shift):
    average = jnp.mean(inputs, axis=-1, keepdims=True)
    centred = inputs - average
    variance = jnp.mean(centred * centred, axis=-1, keepdims=True)
    return centred * lax.rsqrt(variance + epsilon) * norm_gain + norm_shift


def document_ids(document_length_list, seq_len):
    starts = jnp.cumsum(document_length_list, axis=-1) - document_length_list
    places = jnp.arange(seq_len, dtype=jnp.int32)
    reached = places[:, None] >= starts[..., None, :]
    return jnp.sum(reached.astype(jnp.int32), axis=-1)


def block_mask(documents, places, first_row, block_rows):
    row_docs = lax.dynamic_slice_in_dim(documents, first_row, block_rows, 0)
    row_places = first_row + jnp.arange(block_rows, dtype=jnp.int32)
    return (row_docs[:, None] == documents[None, :]) & (places[None, :] <= row_places[:, None])


def attend_slot(query_rows, key_rows, value_vectors, documents):
    seq_len = query_rows.shape[0]
    block_rows = min(512, seq_len)
    block_count = seq_len // block_rows
    places = jnp.arange(seq_len, dtype=jnp.int32)
    score_scale = HEAD_DIM ** (-0.5)

    def one_block(block_idx):
        first_row = block_idx * block_rows
        query_block = lax.dynamic_slice_in_dim(query_rows, first_row, block_rows, 0)
        allowed = block_mask(documents, places, first_row, block_rows)
        scores = (
            jnp.einsum("qhd,khd->hqk", query_block, key_rows, preferred_element_type=jnp.float32)
            * score_scale
        )
        masked = jnp.where(allowed[None], scores, masked_fill)
        highest = jnp.max(masked, axis=-1, keepdims=True)
        exponent = jnp.exp(masked - highest)
        row_total = jnp.sum(exponent, axis=-1, keepdims=True)
        prob_low = (exponent / row_total).astype(jnp.bfloat16)
        result = jnp.einsum(
            "hqk,khd->qhd", prob_low, value_vectors, preferred_element_type=jnp.float32
        )
        return (result, (highest + jnp.log(row_total))[..., 0])

    results, lse_all = lax.map(one_block, jnp.arange(block_count, dtype=jnp.int32))
    return (results.reshape(query_rows.shape), lse_all)


def attend_back(query_rows, key_rows, value_vectors, grad_out, lse_all, documents):
    seq_len = query_rows.shape[0]
    block_rows = min(512, seq_len)
    block_count = seq_len // block_rows
    places = jnp.arange(seq_len, dtype=jnp.int32)
    score_scale = HEAD_DIM ** (-0.5)

    def one_block(running_offset, inputs_pair):
        key_sum, value_sum = running_offset
        block_idx, lse_row = inputs_pair
        first_row = block_idx * block_rows
        query_block = lax.dynamic_slice_in_dim(query_rows, first_row, block_rows, 0)
        grad_block = lax.dynamic_slice_in_dim(grad_out, first_row, block_rows, 0)
        allowed = block_mask(documents, places, first_row, block_rows)
        scores = (
            jnp.einsum("qhd,khd->hqk", query_block, key_rows, preferred_element_type=jnp.float32)
            * score_scale
        )
        masked = jnp.where(allowed[None], scores, masked_fill)
        probs = jnp.exp(masked - lse_row[..., None])
        prob_low = probs.astype(jnp.bfloat16)
        grad_probs = jnp.einsum(
            "qhd,khd->hqk", grad_block, value_vectors, preferred_element_type=jnp.float32
        )
        row_delta = jnp.sum(grad_probs * probs, axis=-1, keepdims=True)
        grad_scores = (probs * (grad_probs - row_delta)).astype(jnp.bfloat16)
        grad_query = (
            jnp.einsum("hqk,khd->qhd", grad_scores, key_rows, preferred_element_type=jnp.float32)
            * score_scale
        )
        key_part = (
            jnp.einsum("hqk,qhd->khd", grad_scores, query_block, preferred_element_type=jnp.float32)
            * score_scale
        )
        value_part = jnp.einsum(
            "hqk,qhd->khd", prob_low, grad_block, preferred_element_type=jnp.float32
        )
        return ((key_sum + key_part, value_sum + value_part), grad_query)

    empty_grad = jnp.zeros(query_rows.shape, jnp.float32)
    (key_grad, value_grad), query_grads = lax.scan(
        one_block, (empty_grad, empty_grad), (jnp.arange(block_count, dtype=jnp.int32), lse_all)
    )
    return (query_grads.reshape(query_rows.shape), key_grad, value_grad)


def forward_pass(slot_rows, documents, frozen_weights, adapter_list):
    (
        joint_projection_weight,
        attention_out_weight,
        feed_up_weight,
        feed_down_weight,
        frozen_norm_gains,
        biases,
        hidden_up_bias,
    ) = frozen_weights
    query_down_adapter, query_up_adapter, value_down_adapter, value_up_adapter = adapter_list
    slot_count, seq_len, feature_width = slot_rows.shape
    token_count = slot_count * seq_len
    gains_full = frozen_norm_gains.astype(jnp.float32)
    biases_full = biases.astype(jnp.float32)
    token_rows = slot_rows.reshape(token_count, feature_width).astype(jnp.float32)
    normalized_rows = layer_norm(token_rows, gains_full[0], biases_full[0]).astype(jnp.bfloat16)
    query_narrow = jnp.dot(
        normalized_rows, query_down_adapter, preferred_element_type=jnp.float32
    ).astype(jnp.bfloat16)
    value_narrow = jnp.dot(
        normalized_rows, value_down_adapter, preferred_element_type=jnp.float32
    ).astype(jnp.bfloat16)
    attention_mixed = jnp.dot(
        normalized_rows, joint_projection_weight, preferred_element_type=jnp.float32
    )
    query_vectors = (
        attention_mixed[:, :feature_width]
        + biases_full[2]
        + adapter_scale
        * jnp.dot(query_narrow, query_up_adapter, preferred_element_type=jnp.float32)
    ).astype(jnp.bfloat16)
    key_rows = attention_mixed[:, feature_width : 2 * feature_width].astype(jnp.bfloat16)
    value_vectors = (
        attention_mixed[:, 2 * feature_width :]
        + biases_full[3]
        + adapter_scale
        * jnp.dot(value_narrow, value_up_adapter, preferred_element_type=jnp.float32)
    ).astype(jnp.bfloat16)
    four_way = (slot_count, seq_len, HEADS, HEAD_DIM)
    query_four = query_vectors.reshape(four_way)
    keys_four = key_rows.reshape(four_way)
    values_four = value_vectors.reshape(four_way)
    attended, lse_all = lax.map(
        lambda packed: attend_slot(*packed), (query_four, keys_four, values_four, documents)
    )
    attended = attended.reshape(token_count, feature_width).astype(jnp.bfloat16)
    hidden_one = (
        token_rows
        + jnp.dot(attended, attention_out_weight, preferred_element_type=jnp.float32)
        + biases_full[4]
    )
    normed_two = layer_norm(hidden_one, gains_full[1], biases_full[1]).astype(jnp.bfloat16)
    pre_act = jnp.dot(
        normed_two, feed_up_weight, preferred_element_type=jnp.float32
    ) + hidden_up_bias.astype(jnp.float32)
    activated = jax.nn.gelu(pre_act, approximate=True).astype(jnp.bfloat16)
    result = (
        hidden_one
        + jnp.dot(activated, feed_down_weight, preferred_element_type=jnp.float32)
        + biases_full[5]
    )
    saved = (
        token_rows,
        normalized_rows,
        query_narrow,
        value_narrow,
        query_four,
        keys_four,
        values_four,
        lse_all,
        hidden_one,
        pre_act,
    )
    return (result.reshape(slot_count, seq_len, feature_width).astype(jnp.bfloat16), saved)


def reverse_sweep(row_gradients, documents, frozen_weights, adapter_list, saved):
    (
        joint_projection_weight,
        attention_out_weight,
        feed_up_weight,
        feed_down_weight,
        frozen_norm_gains,
        biases,
        hidden_up_bias,
    ) = frozen_weights
    query_down_adapter, query_up_adapter, value_down_adapter, value_up_adapter = adapter_list
    (
        token_rows,
        normalized_rows,
        query_narrow,
        value_narrow,
        query_four,
        keys_four,
        values_four,
        lse_all,
        hidden_one,
        pre_act,
    ) = saved
    slot_count, seq_len, feature_width = row_gradients.shape
    token_count = slot_count * seq_len
    gains_full = frozen_norm_gains.astype(jnp.float32)
    biases_full = biases.astype(jnp.float32)
    grad_low = row_gradients.reshape(token_count, feature_width)
    grad_out = grad_low.astype(jnp.float32)
    grad_act = jnp.dot(grad_low, feed_down_weight.T, preferred_element_type=jnp.float32)
    unused, gelu_back = jax.vjp(lambda inputs: jax.nn.gelu(inputs, approximate=True), pre_act)
    grad_pre = gelu_back(grad_act)[0].astype(jnp.bfloat16)
    grad_normed_two = jnp.dot(grad_pre, feed_up_weight.T, preferred_element_type=jnp.float32)
    unused, second_back = jax.vjp(
        lambda inputs: layer_norm(inputs, gains_full[1], biases_full[1]), hidden_one
    )
    grad_hidden = grad_out + second_back(grad_normed_two)[0]
    grad_attended = jnp.dot(
        grad_hidden.astype(jnp.bfloat16), attention_out_weight.T, preferred_element_type=jnp.float32
    ).astype(jnp.bfloat16)
    grad_four = grad_attended.reshape(slot_count, seq_len, HEADS, HEAD_DIM)
    grad_query, grad_keys, grad_values = lax.map(
        lambda packed: attend_back(*packed),
        (query_four, keys_four, values_four, grad_four, lse_all, documents),
    )
    grad_mixed = jnp.concatenate(
        [
            grad_query.reshape(token_count, feature_width),
            grad_keys.reshape(token_count, feature_width),
            grad_values.reshape(token_count, feature_width),
        ],
        axis=1,
    ).astype(jnp.bfloat16)
    query_row_gradient = grad_mixed[:, :feature_width]
    value_row_gradient = grad_mixed[:, 2 * feature_width :]
    query_narrow_gradient = (
        adapter_scale
        * jnp.dot(query_row_gradient, query_up_adapter.T, preferred_element_type=jnp.float32)
    ).astype(jnp.bfloat16)
    value_narrow_gradient = (
        adapter_scale
        * jnp.dot(value_row_gradient, value_up_adapter.T, preferred_element_type=jnp.float32)
    ).astype(jnp.bfloat16)
    query_up_gradient = adapter_scale * jnp.dot(
        query_narrow.T, query_row_gradient, preferred_element_type=jnp.float32
    )
    value_up_gradient = adapter_scale * jnp.dot(
        value_narrow.T, value_row_gradient, preferred_element_type=jnp.float32
    )
    grad_a_q = jnp.dot(normalized_rows.T, query_narrow_gradient, preferred_element_type=jnp.float32)
    grad_a_v = jnp.dot(normalized_rows.T, value_narrow_gradient, preferred_element_type=jnp.float32)
    normalized_gradient = jnp.dot(
        grad_mixed, joint_projection_weight.T, preferred_element_type=jnp.float32
    )
    normalized_gradient = normalized_gradient + jnp.dot(
        query_narrow_gradient, query_down_adapter.T, preferred_element_type=jnp.float32
    )
    normalized_gradient = normalized_gradient + jnp.dot(
        value_narrow_gradient, value_down_adapter.T, preferred_element_type=jnp.float32
    )
    unused, first_back = jax.vjp(
        lambda inputs: layer_norm(inputs, gains_full[0], biases_full[0]), token_rows
    )
    input_gradient_rows = grad_hidden + first_back(normalized_gradient)[0]
    return (
        input_gradient_rows.reshape(slot_count, seq_len, feature_width).astype(jnp.bfloat16),
        (grad_a_q, query_up_gradient, grad_a_v, value_up_gradient),
    )


def per_device(
    tokens,
    document_length_list,
    joint_projection_weight,
    attention_out_weight,
    feed_up_weight,
    feed_down_weight,
    frozen_norm_gains,
    biases,
    hidden_up_bias,
    query_down_adapter,
    query_up_adapter,
    value_down_adapter,
    value_up_adapter,
    cotangent,
):
    shards = (
        joint_projection_weight,
        attention_out_weight,
        feed_up_weight,
        feed_down_weight,
        frozen_norm_gains,
        biases,
        hidden_up_bias,
    )
    adapter_list = (query_down_adapter, query_up_adapter, value_down_adapter, value_up_adapter)
    micro_count = tokens.shape[0]
    seq_len = tokens.shape[2]
    documents = document_ids(document_length_list, seq_len)
    block_outs = []
    input_grads = []
    running_offset = tuple(
        (jnp.zeros(bundle_member.shape, jnp.float32) for bundle_member in adapter_list)
    )
    for section in range(micro_count):
        early_set = (
            lax.all_gather(shards[0], "fsdp", axis=0, tiled=True),
            lax.all_gather(shards[1], "fsdp", axis=0, tiled=True),
            lax.all_gather(shards[2], "fsdp", axis=0, tiled=True),
            lax.all_gather(shards[3], "fsdp", axis=0, tiled=True),
            lax.all_gather(shards[4], "fsdp", axis=1, tiled=True),
            lax.all_gather(shards[5], "fsdp", axis=1, tiled=True),
            lax.all_gather(shards[6], "fsdp", axis=0, tiled=True),
        )
        result, unused_saved = forward_pass(
            tokens[section], documents[section], early_set, adapter_list
        )
        later_set = (
            lax.all_gather(shards[0], "fsdp", axis=0, tiled=True),
            lax.all_gather(shards[1], "fsdp", axis=0, tiled=True),
            lax.all_gather(shards[2], "fsdp", axis=0, tiled=True),
            lax.all_gather(shards[3], "fsdp", axis=0, tiled=True),
            lax.all_gather(shards[4], "fsdp", axis=1, tiled=True),
            lax.all_gather(shards[5], "fsdp", axis=1, tiled=True),
            lax.all_gather(shards[6], "fsdp", axis=0, tiled=True),
        )
        unused_out, saved = forward_pass(
            tokens[section], documents[section], later_set, adapter_list
        )
        input_gradient_rows, adapter_gradients = reverse_sweep(
            cotangent[section], documents[section], later_set, adapter_list, saved
        )
        block_outs.append(result)
        input_grads.append(input_gradient_rows)
        running_offset = tuple(
            (total_length + part for total_length, part in zip(running_offset, adapter_gradients))
        )
    running_offset = lax.psum(running_offset, ("dp", "fsdp"))
    return (
        jnp.stack(block_outs, axis=0),
        jnp.stack(input_grads, axis=0),
        running_offset[0],
        running_offset[1],
        running_offset[2],
        running_offset[3],
    )


def solution(mesh):
    return jax.shard_map(
        per_device,
        mesh=mesh,
        in_specs=(
            P(None, ("dp", "fsdp"), None, None),
            P(None, ("dp", "fsdp"), None),
            P("fsdp", None),
            P("fsdp", None),
            P("fsdp", None),
            P("fsdp", None),
            P(None, "fsdp"),
            P(None, "fsdp"),
            P("fsdp"),
            P(),
            P(),
            P(),
            P(),
            P(None, ("dp", "fsdp"), None, None),
        ),
        out_specs=(
            P(None, ("dp", "fsdp"), None, None),
            P(None, ("dp", "fsdp"), None, None),
            P(),
            P(),
            P(),
            P(),
        ),
        check_vma=False,
    )
```

profile of v0, /device:TPU:0, one launch (start us, length us, event | category | flops | bytes accessed | tf_op | source)
XLA Modules:
  0.0 1515.2 jit_solution(9146052900682985586)
XLA Ops:
  117.6 142.1 %while.133 = (s32[]{:T(128)}, bf16[2,512,16,64]{1,3,2,0:T(8,128)(2,1)}, s32[2]{0:T(128)S(1)}, s32[1024]{0:T(1024)S(1)}, bf16[1024,16,64]{0,2,1:T(8,128)(2,1)}, /...) while((s32[]{:T(128)}, ...), condition=%wide.region_15.16_spmd.clone, body=%wide.region_12.15_spmd.clone.sunk | while | flops 2216166912 | bytes 142686416 | solution.py:60
  119.1 14.7 fusion.465
  134.4 38.9 %fusion.467 = (f32[16,512]{1,0:T(8,128)S(1)}, f32[16,512,1024]{2,1,0:T(8,128)}) fusion(f32[16,512,1024]{2,1,0:T(8,128)} %fusion.465, pred[512,1024]{1,0:T(8,128)(4,1)S(1)} %fusion.466), kind=kOutput, calls=%fused_computation.357.clone.1 | output fusion | flops 50332672 | bytes 67665920 | tf_op jit(solution)/shard_map/while/body/eval_jaxpr/while/body/eval_jaxpr/sub | solution.py:52
  173.3 15.0 bitcast_dynamic-update-slice_fusion.17
  189.6 15.7 %fusion.465 = f32[16,512,1024]{2,1,0:T(8,128)} fusion(bf16[1024,16,64]{0,2,1:T(8,128)(2,1)S(1)} %get-tuple-element.1212, bf16[1024,16,64]{0,2,1:T(8,128)(2,1)} %get-tuple-element.1211, s32[]{:T(128)S(6)} %select_n.144), kind=kOutput, calls=%fused_computation.36.clone.1 | convolution fusion | flops 1073741824 | bytes 36700164 | tf_op jit(solution)/shard_map/while/body/eval_jaxpr/while/body/eval_jaxpr/qhd,khd->hqk/dot_general | solution.py:47
  205.9 38.7 %fusion.467 = (f32[16,512]{1,0:T(8,128)S(1)}, f32[16,512,1024]{2,1,0:T(8,128)}) fusion(f32[16,512,1024]{2,1,0:T(8,128)} %fusion.465, pred[512,1024]{1,0:T(8,128)(4,1)S(1)} %fusion.466), kind=kOutput, calls=%fused_computation.357.clone.1 | output fusion | flops 50332672 | bytes 67665920 | tf_op jit(solution)/shard_map/while/body/eval_jaxpr/while/body/eval_jaxpr/sub | solution.py:52
  244.7 15.0 bitcast_dynamic-update-slice_fusion.17
  291.1 98.0 %while.134 = (s32[]{:T(128)}, bf16[2,512,16,64]{1,3,2,0:T(8,128)(2,1)}, f32[2,16,512]{2,1,0:T(8,128)S(1)}, s32[2]{0:T(128)S(1)}, s32[1024]{0:T(1024)S(1)}, /*ind...) while((s32[]{:T(128)}, ...), condition=%wide.region_21.22_spmd.clone, body=%wide.region_18.21_spmd.clone.sunk | while | flops 2249712128 | bytes 135543056 | solution.py:60
  293.2 15.6 %fusion.471 = (f32[16,512]{1,0:T(8,128)S(1)}, f32[16,512,1024]{2,1,0:T(8,128)}) fusion(pred[512,1024]{1,0:T(8,128)(4,1)S(1)} %fusion.470, bf16[1024,16,64]{0,2,1:T(8,128)(2,1)} %get-tuple-element.1281, bf16[1024,16,64]{0,2,1:T(8,128)(2,1)} %get-tuple-element.1280, s32[]{:T(128)S(6)} %select_n.148), kind=kOutput, calls=%fused_computation.45.clone.1 | convolution fusion | flops 1098899456 | bytes 37257220 | tf_op jit(solution)/shard_map/while/body/eval_jaxpr/while/body/eval_jaxpr/qhd,khd->hqk/dot_general | solution.py:47
  308.9 15.3 %fusion.472 = f32[16,512]{1,0:T(8,128)S(1)} fusion(f32[16,512,1024]{2,1,0:T(8,128)} %get-tuple-element.1147, f32[16,512]{1,0:T(8,128)S(1)} %get-tuple-element.1148, pred[512,1024]{1,0:T(8,128)(4,1)S(1)} %fusion.470), kind=kLoop, calls=%fused_computation.46.clone.1 | loop fusion | flops 33546240 | bytes 34144256 | tf_op jit(solution)/shard_map/while/body/eval_jaxpr/while/body/eval_jaxpr/reduce_sum | solution.py:53
  324.2 14.7 bitcast_dynamic-update-slice_fusion.18
  342.1 15.6 %fusion.471 = (f32[16,512]{1,0:T(8,128)S(1)}, f32[16,512,1024]{2,1,0:T(8,128)}) fusion(pred[512,1024]{1,0:T(8,128)(4,1)S(1)} %fusion.470, bf16[1024,16,64]{0,2,1:T(8,128)(2,1)} %get-tuple-element.1281, bf16[1024,16,64]{0,2,1:T(8,128)(2,1)} %get-tuple-element.1280, s32[]{:T(128)S(6)} %select_n.148), kind=kOutput, calls=%fused_computation.45.clone.1 | convolution fusion | flops 1098899456 | bytes 37257220 | tf_op jit(solution)/shard_map/while/body/eval_jaxpr/while/body/eval_jaxpr/qhd,khd->hqk/dot_general | solution.py:47
  357.8 15.3 %fusion.472 = f32[16,512]{1,0:T(8,128)S(1)} fusion(f32[16,512,1024]{2,1,0:T(8,128)} %get-tuple-element.1147, f32[16,512]{1,0:T(8,128)S(1)} %get-tuple-element.1148, pred[512,1024]{1,0:T(8,128)(4,1)S(1)} %fusion.470), kind=kLoop, calls=%fused_computation.46.clone.1 | loop fusion | flops 33546240 | bytes 34144256 | tf_op jit(solution)/shard_map/while/body/eval_jaxpr/while/body/eval_jaxpr/reduce_sum | solution.py:53
  373.1 14.7 bitcast_dynamic-update-slice_fusion.18
  390.7 97.4 %while.135 = (s32[]{:T(128)}, bf16[2,512,16,64]{1,3,2,0:T(8,128)(2,1)}, f32[2,16,512]{2,1,0:T(8,128)S(1)}, s32[2]{0:T(128)S(1)}, s32[1024]{0:T(1024)S(1)}, /*ind...) while((s32[]{:T(128)}, ...), condition=%wide.region_34.35_spmd.clone, body=%wide.region_31.34_spmd.clone.sunk | while | flops 2249712128 | bytes 135543056 | solution.py:60
  392.9 15.4 %fusion.476 = (f32[16,512]{1,0:T(8,128)S(1)}, f32[16,512,1024]{2,1,0:T(8,128)}) fusion(pred[512,1024]{1,0:T(8,128)(4,1)S(1)} %fusion.475, bf16[1024,16,64]{0,2,1:T(8,128)(2,1)S(1)} %get-tuple-element.1317, bf16[1024,16,64]{0,2,1:T(8,128)(2,1)} %get-tuple-element.1316, s32[]{:T(128)S(6)} %select_n.152), kind=kOutput, calls=%fused_computation.61.clone.1 | convolution fusion | flops 1098899456 | bytes 37257220 | tf_op jit(solution)/shard_map/while/body/eval_jaxpr/while/body/eval_jaxpr/qhd,khd->hqk/dot_general | solution.py:47
  408.2 15.3 %fusion.477 = f32[16,512]{1,0:T(8,128)S(1)} fusion(f32[16,512,1024]{2,1,0:T(8,128)} %get-tuple-element.1157, f32[16,512]{1,0:T(8,128)S(1)} %get-tuple-element.1158, pred[512,1024]{1,0:T(8,128)(4,1)S(1)} %fusion.475), kind=kLoop, calls=%fused_computation.62.clone.1 | loop fusion | flops 33546240 | bytes 34144256 | tf_op jit(solution)/shard_map/while/body/eval_jaxpr/while/body/eval_jaxpr/reduce_sum | solution.py:53
  423.6 14.7 bitcast_dynamic-update-slice_fusion.20
  441.5 15.4 %fusion.476 = (f32[16,512]{1,0:T(8,128)S(1)}, f32[16,512,1024]{2,1,0:T(8,128)}) fusion(pred[512,1024]{1,0:T(8,128)(4,1)S(1)} %fusion.475, bf16[1024,16,64]{0,2,1:T(8,128)(2,1)S(1)} %get-tuple-element.1317, bf16[1024,16,64]{0,2,1:T(8,128)(2,1)} %get-tuple-element.1316, s32[]{:T(128)S(6)} %select_n.152), kind=kOutput, calls=%fused_computation.61.clone.1 | convolution fusion | flops 1098899456 | bytes 37257220 | tf_op jit(solution)/shard_map/while/body/eval_jaxpr/while/body/eval_jaxpr/qhd,khd->hqk/dot_general | solution.py:47
  456.8 15.3 %fusion.477 = f32[16,512]{1,0:T(8,128)S(1)} fusion(f32[16,512,1024]{2,1,0:T(8,128)} %get-tuple-element.1157, f32[16,512]{1,0:T(8,128)S(1)} %get-tuple-element.1158, pred[512,1024]{1,0:T(8,128)(4,1)S(1)} %fusion.475), kind=kLoop, calls=%fused_computation.62.clone.1 | loop fusion | flops 33546240 | bytes 34144256 | tf_op jit(solution)/shard_map/while/body/eval_jaxpr/while/body/eval_jaxpr/reduce_sum | solution.py:53
  472.1 14.7 bitcast_dynamic-update-slice_fusion.20
  489.7 144.8 %while.132 = (s32[]{:T(128)}, bf16[2,512,16,64]{1,3,2,0:T(8,128)(2,1)}, s32[2]{0:T(128)S(1)}, s32[1024]{0:T(1024)S(1)}, bf16[1024,16,64]{0,2,1:T(8,128)(2,1)}, /...) while((s32[]{:T(128)}, ...), condition=%wide.region_7.8_spmd.clone, body=%wide.region_4.7_spmd.clone.sunk | while | flops 2216166912 | bytes 151075056 | solution.py:60
  491.2 17.5 %fusion.459 = f32[16,512,1024]{2,1,0:T(8,128)} fusion(bf16[1024,16,64]{0,2,1:T(8,128)(2,1)} %get-tuple-element.1245, bf16[1024,16,64]{0,2,1:T(8,128)(2,1)} %get-tuple-element.1244, s32[]{:T(128)S(6)} %select_n.142), kind=kOutput, calls=%fused_computation.18.clone.1 | convolution fusion | flops 1073741824 | bytes 36700164 | tf_op jit(solution)/shard_map/while/body/eval_jaxpr/while/body/eval_jaxpr/qhd,khd->hqk/dot_general | solution.py:47
  509.4 38.5 %fusion.461 = (f32[16,512]{1,0:T(8,128)S(1)}, f32[16,512,1024]{2,1,0:T(8,128)}) fusion(f32[16,512,1024]{2,1,0:T(8,128)} %fusion.459, pred[512,1024]{1,0:T(8,128)(4,1)S(1)} %fusion.460), kind=kOutput, calls=%fused_computation.356.clone.1 | output fusion | flops 50332672 | bytes 67665920 | tf_op jit(solution)/shard_map/while/body/eval_jaxpr/while/body/eval_jaxpr/sub | solution.py:52
  563.3 17.5 %fusion.459 = f32[16,512,1024]{2,1,0:T(8,128)} fusion(bf16[1024,16,64]{0,2,1:T(8,128)(2,1)} %get-tuple-element.1245, bf16[1024,16,64]{0,2,1:T(8,128)(2,1)} %get-tuple-element.1244, s32[]{:T(128)S(6)} %select_n.142), kind=kOutput, calls=%fused_computation.18.clone.1 | convolution fusion | flops 1073741824 | bytes 36700164 | tf_op jit(solution)/shard_map/while/body/eval_jaxpr/while/body/eval_jaxpr/qhd,khd->hqk/dot_general | solution.py:47
  581.5 38.5 %fusion.461 = (f32[16,512]{1,0:T(8,128)S(1)}, f32[16,512,1024]{2,1,0:T(8,128)}) fusion(f32[16,512,1024]{2,1,0:T(8,128)} %fusion.459, pred[512,1024]{1,0:T(8,128)(4,1)S(1)} %fusion.460), kind=kOutput, calls=%fused_computation.356.clone.1 | output fusion | flops 50332672 | bytes 67665920 | tf_op jit(solution)/shard_map/while/body/eval_jaxpr/while/body/eval_jaxpr/sub | solution.py:52
  675.5 16.7 %fusion.198 = f32[1024,4096]{1,0:T(8,128)} fusion(bf16[4096,1024]{1,0:T(8,128)(2,1)} %all-gather.12.cloned.1.call-done, bf16[2,1,1024,1024]{3,2,1,0:T(8,128)(2,1)} %param.39), kind=kOutput, calls=%fused_computation.256 | convolution fusion | flops 8589934592 | bytes 27262976 | tf_op jit(solution)/shard_map/dot_general | solution.py:216
  706.8 28.2 %fusion.408 = bf16[1024,4096]{1,0:T(8,128)(2,1)} fusion(f32[1024,4096]{1,0:T(8,128)} %fusion.198, f32[4096]{0:T(1024)S(1)} %bitcast.423, bf16[1024,4096]{1,0:T(8,128)(2,1)} %all-gather.10.cloned.1.call-done, f32[1024,1024]{0,1:T(8,128)} %copy-done.35, f32[1024]{0:T(1024)S(1)} %fusion.261, f32[1024]{0:T(1024)S(1)} %broadcast_multiply_fusion, ...), kind=kOutput, calls=%fused_computation.143.clone.clone.1 | convolution fusion | flops 8683257856 | bytes 37781504 | tf_op jit(solution)/shard_map/dot_general | solution.py:163
  735.0 15.3 %fusion.130 = f32[1024,1024]{0,1:T(8,128)} fusion(bf16[1024,4096]{1,0:T(8,128)(2,1)} %all-gather.10.cloned.1.call-done, bf16[1024,4096]{1,0:T(8,128)(2,1)} %fusion.408), kind=kOutput, calls=%fused_computation.164 | convolution fusion | flops 8589934592 | bytes 20971520 | tf_op jit(solution)/shard_map/dot_general | solution.py:219
  750.3 27.0 %fusion.135.clone.4 = bf16[1024,4096]{1,0:T(8,128)(2,1)} fusion(f32[1024,4096]{1,0:T(8,128)} %fusion.200, f32[4096]{0:T(1024)S(1)} %bitcast.424, bf16[1024,4096]{1,0:T(8,128)(2,1)} %all-gather.10.cloned.1.call-done, f32[1024,1024]{0,1:T(8,128)S(1)} %copy-done.34, f32[1024]{0:T(1024)S(1)} %fusion.260, ...), kind=kOutput, calls=%fused_computation.136.clone.clone.clone.clone.1 | convolution fusion | flops 8683257856 | bytes 37781504 | tf_op jit(solution)/shard_map/dot_general | solution.py:163
  777.3 18.1 %multiply_reduce_fusion.4 = (f32[1024]{0:T(1024)S(1)}, f32[1024]{0:T(1024)S(1)}, f32[1024,1024]{0,1:T(8,128)}) fusion(f32[1024,1024]{0,1:T(8,128)S(1)} %copy-done.34, f32[1024]{0:T(1024)S(1)} %broadcast_multiply_fusion.1, f32[1024]{0:T(1024)S(1)} %bitcast.429, f32[1024,1024]{0,1:T(8,128)} %fusion.130, f32[1024,1024]{0,1:T(8,128)} %copy-done.35, ...), kind=kOutput, calls=%fused_computation.241 | convolution fusion | flops 8598321152 | bytes 33574912 | tf_op jit(solution)/shard_map/dot_general | solution.py:219
  807.3 219.3 %while.136 = (s32[]{:T(128)}, f32[1024,16,64]{0,2,1:T(8,128)}, f32[1024,16,64]{0,2,1:T(8,128)}, bf16[2,512,16,64]{1,3,2,0:T(8,128)(2,1)}, s32[2]{0:T(128)S(1)}, ...) while((s32[]{:T(128)}, f32[1024,16,64]{0,2,1:T(8,128)}, ...), condition=%wide.region_28.29_spmd.clone, body=%wide.region_26.28_spmd.clone.sunk | while | flops 5501870592 | bytes 300136736 | solution.py:104
  824.0 25.5 %multiply_reduce_fusion.10 = (f32[16,512]{1,0:T(8,128)S(1)}, f32[16,512,1024]{2,1,0:T(8,128)}) fusion(f32[16,512,1024]{2,1,0:T(8,128)} %fusion.487, f32[16,512]{1,0:T(8,128)S(1)} %dynamic-slice_bitcast_fusion.4, pred[512,1024]{1,0:T(8,128)(4,1)S(1)} %fusion.488, bf16[1024,16,64]{0,2,1:T(8,128)(2,1)S(1)} %copy-done.11, ...), kind=kOutput, calls=%fused_computation.75.clone.1 | convolution fusion | flops 1115676672 | bytes 70844416 | tf_op jit(solution)/shard_map/while/body/eval_jaxpr/while/body/eval_jaxpr/qhd,khd->hqk/dot_general | solution.py:85
  849.5 27.8 %multiply_convert_fusion.4 = bf16[16,512,1024]{2,1,0:T(8,128)(2,1)} fusion(f32[16,512,1024]{2,1,0:T(8,128)} %get-tuple-element.1170, f32[16,512,1024]{2,1,0:T(8,128)} %fusion.487, f32[16,512]{1,0:T(8,128)S(1)} %get-tuple-element.1171, f32[16,512]{1,0:T(8,128)S(1)} %dynamic-slice_bitcast_fusion.4, pred[512,1024]{1,0:T(8,128)(4,1)S(1)} %fusion.488), kind=kLoop, calls=%fused_computation.74.clone.1 | loop fusion | flops 50331648 | bytes 84475904 | tf_op jit(solution)/shard_map/while/body/eval_jaxpr/while/body/eval_jaxpr/convert_element_type | solution.py:89
  888.4 17.5 %bitcast_add_fusion.9 = f32[1024,16,64]{0,2,1:T(8,128)} fusion(f32[1024,16,64]{0,2,1:T(8,128)} %get-tuple-element.1385, f32[16,512,1024]{2,1,0:T(8,128)} %fusion.487, f32[16,512]{1,0:T(8,128)S(1)} %dynamic-slice_bitcast_fusion.4, pred[512,1024]{1,0:T(8,128)(4,1)S(1)} %fusion.488, pred[]{:T(512)S(6)} %compare.6, ...), kind=kOutput, calls=%fused_computation.80.clone.1 | convolution fusion | flops 1109393408 | bytes 43548676 | tf_op jit(solution)/shard_map/while/body/eval_jaxpr/while/body/eval_jaxpr/hqk,qhd->khd/dot_general | solution.py:98
  932.2 25.5 %multiply_reduce_fusion.10 = (f32[16,512]{1,0:T(8,128)S(1)}, f32[16,512,1024]{2,1,0:T(8,128)}) fusion(f32[16,512,1024]{2,1,0:T(8,128)} %fusion.487, f32[16,512]{1,0:T(8,128)S(1)} %dynamic-slice_bitcast_fusion.4, pred[512,1024]{1,0:T(8,128)(4,1)S(1)} %fusion.488, bf16[1024,16,64]{0,2,1:T(8,128)(2,1)S(1)} %copy-done.11, ...), kind=kOutput, calls=%fused_computation.75.clone.1 | convolution fusion | flops 1115676672 | bytes 70844416 | tf_op jit(solution)/shard_map/while/body/eval_jaxpr/while/body/eval_jaxpr/qhd,khd->hqk/dot_general | solution.py:85
  957.7 27.8 %multiply_convert_fusion.4 = bf16[16,512,1024]{2,1,0:T(8,128)(2,1)} fusion(f32[16,512,1024]{2,1,0:T(8,128)} %get-tuple-element.1170, f32[16,512,1024]{2,1,0:T(8,128)} %fusion.487, f32[16,512]{1,0:T(8,128)S(1)} %get-tuple-element.1171, f32[16,512]{1,0:T(8,128)S(1)} %dynamic-slice_bitcast_fusion.4, pred[512,1024]{1,0:T(8,128)(4,1)S(1)} %fusion.488), kind=kLoop, calls=%fused_computation.74.clone.1 | loop fusion | flops 50331648 | bytes 84475904 | tf_op jit(solution)/shard_map/while/body/eval_jaxpr/while/body/eval_jaxpr/convert_element_type | solution.py:89
  997.8 18.7 %bitcast_add_fusion.9 = f32[1024,16,64]{0,2,1:T(8,128)} fusion(f32[1024,16,64]{0,2,1:T(8,128)} %get-tuple-element.1385, f32[16,512,1024]{2,1,0:T(8,128)} %fusion.487, f32[16,512]{1,0:T(8,128)S(1)} %dynamic-slice_bitcast_fusion.4, pred[512,1024]{1,0:T(8,128)(4,1)S(1)} %fusion.488, pred[]{:T(512)S(6)} %compare.6, ...), kind=kOutput, calls=%fused_computation.80.clone.1 | convolution fusion | flops 1109393408 | bytes 43548676 | tf_op jit(solution)/shard_map/while/body/eval_jaxpr/while/body/eval_jaxpr/hqk,qhd->khd/dot_general | solution.py:98
  1046.4 219.4 %while.137 = (s32[]{:T(128)}, f32[1024,16,64]{0,2,1:T(8,128)}, f32[1024,16,64]{0,2,1:T(8,128)}, bf16[2,512,16,64]{1,3,2,0:T(8,128)(2,1)}, s32[2]{0:T(128)S(1)}, ...) while((s32[]{:T(128)}, f32[1024,16,64]{0,2,1:T(8,128)}, ...), condition=%wide.region_41.42_spmd.clone, body=%wide.region_39.41_spmd.clone.sunk | while | flops 5501870592 | bytes 300136736 | solution.py:104
  1063.1 25.5 %multiply_reduce_fusion.11 = (f32[16,512]{1,0:T(8,128)S(1)}, f32[16,512,1024]{2,1,0:T(8,128)}) fusion(f32[16,512,1024]{2,1,0:T(8,128)} %fusion.498, f32[16,512]{1,0:T(8,128)S(1)} %dynamic-slice_bitcast_fusion.5, pred[512,1024]{1,0:T(8,128)(4,1)S(1)} %fusion.499, bf16[1024,16,64]{0,2,1:T(8,128)(2,1)S(1)} %copy-done.8, ...), kind=kOutput, calls=%fused_computation.100.clone.1 | convolution fusion | flops 1115676672 | bytes 70844416 | tf_op jit(solution)/shard_map/while/body/eval_jaxpr/while/body/eval_jaxpr/qhd,khd->hqk/dot_general | solution.py:85
  1088.7 27.8 %multiply_convert_fusion.5 = bf16[16,512,1024]{2,1,0:T(8,128)(2,1)} fusion(f32[16,512,1024]{2,1,0:T(8,128)} %get-tuple-element.1183, f32[16,512,1024]{2,1,0:T(8,128)} %fusion.498, f32[16,512]{1,0:T(8,128)S(1)} %get-tuple-element.1184, f32[16,512]{1,0:T(8,128)S(1)} %dynamic-slice_bitcast_fusion.5, pred[512,1024]{1,0:T(8,128)(4,1)S(1)} %fusion.499), kind=kLoop, calls=%fused_computation.99.clone.1 | loop fusion | flops 50331648 | bytes 84475904 | tf_op jit(solution)/shard_map/while/body/eval_jaxpr/while/body/eval_jaxpr/convert_element_type | solution.py:89
  1127.5 17.5 %bitcast_add_fusion.11 = f32[1024,16,64]{0,2,1:T(8,128)} fusion(f32[1024,16,64]{0,2,1:T(8,128)} %get-tuple-element.1340, f32[16,512,1024]{2,1,0:T(8,128)} %fusion.498, f32[16,512]{1,0:T(8,128)S(1)} %dynamic-slice_bitcast_fusion.5, pred[512,1024]{1,0:T(8,128)(4,1)S(1)} %fusion.499, pred[]{:T(512)S(6)} %compare.7, ...), kind=kOutput, calls=%fused_computation.105.clone.1 | convolution fusion | flops 1109393408 | bytes 43548676 | tf_op jit(solution)/shard_map/while/body/eval_jaxpr/while/body/eval_jaxpr/hqk,qhd->khd/dot_general | solution.py:98
  1171.3 25.5 %multiply_reduce_fusion.11 = (f32[16,512]{1,0:T(8,128)S(1)}, f32[16,512,1024]{2,1,0:T(8,128)}) fusion(f32[16,512,1024]{2,1,0:T(8,128)} %fusion.498, f32[16,512]{1,0:T(8,128)S(1)} %dynamic-slice_bitcast_fusion.5, pred[512,1024]{1,0:T(8,128)(4,1)S(1)} %fusion.499, bf16[1024,16,64]{0,2,1:T(8,128)(2,1)S(1)} %copy-done.8, ...), kind=kOutput, calls=%fused_computation.100.clone.1 | convolution fusion | flops 1115676672 | bytes 70844416 | tf_op jit(solution)/shard_map/while/body/eval_jaxpr/while/body/eval_jaxpr/qhd,khd->hqk/dot_general | solution.py:85
  1196.9 27.8 %multiply_convert_fusion.5 = bf16[16,512,1024]{2,1,0:T(8,128)(2,1)} fusion(f32[16,512,1024]{2,1,0:T(8,128)} %get-tuple-element.1183, f32[16,512,1024]{2,1,0:T(8,128)} %fusion.498, f32[16,512]{1,0:T(8,128)S(1)} %get-tuple-element.1184, f32[16,512]{1,0:T(8,128)S(1)} %dynamic-slice_bitcast_fusion.5, pred[512,1024]{1,0:T(8,128)(4,1)S(1)} %fusion.499), kind=kLoop, calls=%fused_computation.99.clone.1 | loop fusion | flops 50331648 | bytes 84475904 | tf_op jit(solution)/shard_map/while/body/eval_jaxpr/while/body/eval_jaxpr/convert_element_type | solution.py:89
  1236.9 18.7 %bitcast_add_fusion.11 = f32[1024,16,64]{0,2,1:T(8,128)} fusion(f32[1024,16,64]{0,2,1:T(8,128)} %get-tuple-element.1340, f32[16,512,1024]{2,1,0:T(8,128)} %fusion.498, f32[16,512]{1,0:T(8,128)S(1)} %dynamic-slice_bitcast_fusion.5, pred[512,1024]{1,0:T(8,128)(4,1)S(1)} %fusion.499, pred[]{:T(512)S(6)} %compare.7, ...), kind=kOutput, calls=%fused_computation.105.clone.1 | convolution fusion | flops 1109393408 | bytes 43548676 | tf_op jit(solution)/shard_map/while/body/eval_jaxpr/while/body/eval_jaxpr/hqk,qhd->khd/dot_general | solution.py:98
  1317.6 31.5 %fusion.249 = bf16[1,1,1024,1024]{2,3,1,0:T(8,128)(2,1)} fusion(f32[1024]{0:T(1024)S(1)} %bitcast.437, f32[1024,1024]{0,1:T(8,128)} %copy-done.57, bf16[4096,1024]{1,0:T(8,128)(2,1)} %all-gather.12.cloned.1.call-done, f32[4096]{0:T(1024)S(1)} %bitcast.425, bf16[1024,4096]{1,0:T(8,128)(2,1)} %all-gather.10.cloned.1.call-done, f32[1024]{0:T(1024)S(1)} %copy-done.133, ...), kind=kOutput, calls=%fused_computation.285 | convolution fusion | flops 17230200832 | bytes 23105536 | tf_op jit(solution)/shard_map/dot_general | solution.py:169
  1349.1 31.3 %fusion.246 = bf16[1,1,1024,1024]{2,3,1,0:T(8,128)(2,1)} fusion(f32[1024]{0:T(1024)S(1)} %bitcast.438, f32[1024,1024]{0,1:T(8,128)} %copy-done.58, bf16[4096,1024]{1,0:T(8,128)(2,1)} %all-gather.12.cloned.1.call-done, f32[4096]{0:T(1024)S(1)} %bitcast.426, bf16[1024,4096]{1,0:T(8,128)(2,1)} %all-gather.10.cloned.1.call-done, f32[1024]{0:T(1024)S(1)} %bitcast.436, ...), kind=kOutput, calls=%fused_computation.284 | convolution fusion | flops 17230200832 | bytes 23105536 | tf_op jit(solution)/shard_map/dot_general | solution.py:169
  1401.6 101.3 %all-reduce.3.cloned.1.call-done = (f32[1024,4]{0,1:T(4,128)}, f32[4,1024]{1,0:T(4,128)}, f32[1024,4]{0,1:T(4,128)}, f32[4,1024]{1,0:T(4,128)}) async-done(((f32[1024,4]{0,1:T(4,128)}, f32[4,1024]{1,0:T(4,128)}, f32[1024,4]{0,1:T(4,128)}, f32[4,1024]{1,0:T(4,128)}), (f32[1024,4]{0,1:T(4,128)}, f32[4,1024]{1,0:T(4,128)}, f32[1024,4]{0,1:T(4,128)}, f32[4,1024]{1,0:T(4,128)})) %all-reduce.3.cloned.1.call-update) | async-done | bytes 65552 | tf_op jit(solution)/shard_map/psum | solution.py:344
  (526 shorter events, 502.2 us)
Async XLA Ops:
  7.2 50.2 %copy-start = (bf16[1024,4]{0,1:T(4,128)(2,1)S(1)}, bf16[1024,4]{0,1:T(4,128)(2,1)}, u32[]{:S(2)}) copy-start(bf16[1024,4]{0,1:T(4,128)(2,1)} %param.37) | copy-start | bytes 24580
  7.2 80.2 %all-gather.6.cloned.1.call-start = ((), (), s32[]{:S(2)}) async-start(), calls=%async_computation | async-start | bytes 7077888 | tf_op jit(solution)/shard_map/all_gather | solution.py:313
  7.9 644.6 %all-gather.8.cloned.1.call-start = ((), (), s32[]{:S(2)}) async-start(), calls=%async_computation.1 | async-start | bytes 2359296 | tf_op jit(solution)/shard_map/all_gather | solution.py:314
  8.7 666.8 %all-gather.12.cloned.1.call-start = ((), (), s32[]{:S(2)}) async-start(), calls=%async_computation.3 | async-start | bytes 9437184 | tf_op jit(solution)/shard_map/all_gather | solution.py:316
  9.4 697.4 %all-gather.10.cloned.1.call-start = ((), (), s32[]{:S(2)}) async-start(), calls=%async_computation.2 | async-start | bytes 9437184 | tf_op jit(solution)/shard_map/all_gather | solution.py:315
  10.0 1492.9 %all-reduce.3.cloned.1.call-start = ((), (), s32[]{:S(2)}) async-start(), calls=%async_computation.4 | async-start | bytes 131072 | tf_op jit(solution)/shard_map/psum | solution.py:344
  25.2 73.0 %copy-start.113 = (f32[1,1024]{1,0:T(1,128)}, f32[1,1024]{1,0:T(1,128)S(1)}, u32[]{:S(2)}) copy-start(f32[1,1024]{1,0:T(1,128)S(1)} %get-tuple-element.816) | copy-start | bytes 12292
  25.2 82.6 %copy-start.111 = (f32[1,1024]{1,0:T(1,128)}, f32[1,1024]{1,0:T(1,128)S(1)}, u32[]{:S(2)}) copy-start(f32[1,1024]{1,0:T(1,128)S(1)} %get-tuple-element.815) | copy-start | bytes 12292
  32.8 21.3 %copy-start.12 = (bf16[1,1,1024,1024]{2,3,1,0:T(8,128)(2,1)}, bf16[1,1,1024,1024]{2,3,1,0:T(8,128)(2,1)S(1)}, u32[]{:S(2)}) copy-start(bf16[1,1,1024,1024]{2,3,1,0:T(8,128)(2,1)S(1)} %copy.128) | copy-start | bytes 6291460
  44.1 9.9 copy-start.98
  44.5 9.6 copy-start.74
  57.4 40.8 %copy-start.91 = (bf16[1024,4]{0,1:T(4,128)(2,1)}, bf16[1024,4]{0,1:T(4,128)(2,1)S(1)}, u32[]{:S(2)}) copy-start(bf16[1024,4]{0,1:T(4,128)(2,1)S(1)} %convolution_convert_fusion.1) | copy-start | bytes 24580
  57.7 50.1 %copy-start.89 = (bf16[1024,4]{0,1:T(4,128)(2,1)}, bf16[1024,4]{0,1:T(4,128)(2,1)S(1)}, u32[]{:S(2)}) copy-start(bf16[1024,4]{0,1:T(4,128)(2,1)S(1)} %convolution_convert_fusion) | copy-start | bytes 24580
  259.7 10.4 copy-start.1
  259.7 10.4 copy-start.60
  291.1 99.6 %copy-start.2 = (bf16[1024,16,64]{0,2,1:T(8,128)(2,1)S(1)}, bf16[1024,16,64]{0,2,1:T(8,128)(2,1)}, u32[]{:S(2)}) copy-start(bf16[1024,16,64]{0,2,1:T(8,128)(2,1)} %copy-done.1) | copy-start | bytes 6291460
  291.1 99.6 %copy-start.61 = (s32[1024]{0:T(1024)S(1)}, s32[1024]{0:T(1024)}, u32[]{:S(2)}) copy-start(s32[1024]{0:T(1024)} %copy-done.60) | copy-start | bytes 12292
  308.9 15.3 %copy-start.9 = (bf16[1024,16,64]{0,2,1:T(8,128)(2,1)S(1)}, bf16[1024,16,64]{0,2,1:T(8,128)(2,1)}, u32[]{:S(2)}) copy-start(bf16[1024,16,64]{0,2,1:T(8,128)(2,1)} %get-tuple-element.1282) | copy-start | bytes 6291460 | tf_op jit(solution)/shard_map/while/body/eval_jaxpr/while
  308.9 15.3 %copy-start.47 = (bf16[2,512,16,64]{1,3,2,0:T(8,128)(2,1)S(1)}, bf16[2,512,16,64]{1,3,2,0:T(8,128)(2,1)}, u32[]{:S(2)}) copy-start(bf16[2,512,16,64]{1,3,2,0:T(8,128)(2,1)} %get-tuple-element.1264) | copy-start | bytes 6291460 | tf_op jit(solution)/shard_map/while/body/eval_jaxpr/while
  357.8 15.3 %copy-start.9 = (bf16[1024,16,64]{0,2,1:T(8,128)(2,1)S(1)}, bf16[1024,16,64]{0,2,1:T(8,128)(2,1)}, u32[]{:S(2)}) copy-start(bf16[1024,16,64]{0,2,1:T(8,128)(2,1)} %get-tuple-element.1282) | copy-start | bytes 6291460 | tf_op jit(solution)/shard_map/while/body/eval_jaxpr/while
  357.8 15.3 %copy-start.47 = (bf16[2,512,16,64]{1,3,2,0:T(8,128)(2,1)S(1)}, bf16[2,512,16,64]{1,3,2,0:T(8,128)(2,1)}, u32[]{:S(2)}) copy-start(bf16[2,512,16,64]{1,3,2,0:T(8,128)(2,1)} %get-tuple-element.1264) | copy-start | bytes 6291460 | tf_op jit(solution)/shard_map/while/body/eval_jaxpr/while
  390.7 99.0 %copy-start.64 = (s32[1,1024]{1,0:T(1,128)S(1)}, s32[1,1024]{1,0:T(1,128)}, u32[]{:S(2)}) copy-start(s32[1,1024]{1,0:T(1,128)} %get-tuple-element.822) | copy-start | bytes 12292
  408.2 15.3 %copy-start.7 = (bf16[1024,16,64]{0,2,1:T(8,128)(2,1)S(1)}, bf16[1024,16,64]{0,2,1:T(8,128)(2,1)}, u32[]{:S(2)}) copy-start(bf16[1024,16,64]{0,2,1:T(8,128)(2,1)} %get-tuple-element.1318) | copy-start | bytes 6291460 | tf_op jit(solution)/shard_map/while/body/eval_jaxpr/while
  408.2 15.3 %copy-start.50 = (bf16[2,512,16,64]{1,3,2,0:T(8,128)(2,1)S(1)}, bf16[2,512,16,64]{1,3,2,0:T(8,128)(2,1)}, u32[]{:S(2)}) copy-start(bf16[2,512,16,64]{1,3,2,0:T(8,128)(2,1)} %get-tuple-element.1300) | copy-start | bytes 6291460 | tf_op jit(solution)/shard_map/while/body/eval_jaxpr/while
  456.8 15.3 %copy-start.7 = (bf16[1024,16,64]{0,2,1:T(8,128)(2,1)S(1)}, bf16[1024,16,64]{0,2,1:T(8,128)(2,1)}, u32[]{:S(2)}) copy-start(bf16[1024,16,64]{0,2,1:T(8,128)(2,1)} %get-tuple-element.1318) | copy-start | bytes 6291460 | tf_op jit(solution)/shard_map/while/body/eval_jaxpr/while
  456.8 15.3 %copy-start.50 = (bf16[2,512,16,64]{1,3,2,0:T(8,128)(2,1)S(1)}, bf16[2,512,16,64]{1,3,2,0:T(8,128)(2,1)}, u32[]{:S(2)}) copy-start(bf16[2,512,16,64]{1,3,2,0:T(8,128)(2,1)} %get-tuple-element.1300) | copy-start | bytes 6291460 | tf_op jit(solution)/shard_map/while/body/eval_jaxpr/while
  509.4 38.5 %copy-start.10 = (bf16[1024,16,64]{0,2,1:T(8,128)(2,1)S(1)}, bf16[1024,16,64]{0,2,1:T(8,128)(2,1)}, u32[]{:S(2)}) copy-start(bf16[1024,16,64]{0,2,1:T(8,128)(2,1)} %get-tuple-element.1246) | copy-start | bytes 6291460 | tf_op jit(solution)/shard_map/while/body/eval_jaxpr/while
  581.5 38.5 %copy-start.10 = (bf16[1024,16,64]{0,2,1:T(8,128)(2,1)S(1)}, bf16[1024,16,64]{0,2,1:T(8,128)(2,1)}, u32[]{:S(2)}) copy-start(bf16[1024,16,64]{0,2,1:T(8,128)(2,1)} %get-tuple-element.1246) | copy-start | bytes 6291460 | tf_op jit(solution)/shard_map/while/body/eval_jaxpr/while
  675.5 16.7 %copy-start.56 = (bf16[2,1,1024,1024]{3,2,1,0:T(8,128)(2,1)S(1)}, bf16[2,1,1024,1024]{3,2,1,0:T(8,128)(2,1)}, u32[]{:S(2)}) copy-start(bf16[2,1,1024,1024]{3,2,1,0:T(8,128)(2,1)} %param.39) | copy-start | bytes 12582916
  692.2 14.6 copy-start.119
  692.2 14.6 copy-start.126
  692.2 14.6 copy-start.128
  735.0 15.3 %copy-start.34 = (f32[1024,1024]{0,1:T(8,128)S(1)}, f32[1024,1024]{0,1:T(8,128)}, u32[]{:S(2)}) copy-start(f32[1024,1024]{0,1:T(8,128)} %copy-done.33) | copy-start | bytes 12582916
  777.3 18.1 %copy-start.36 = (f32[1024,1024]{0,1:T(8,128)S(1)}, f32[1024,1024]{0,1:T(8,128)}, u32[]{:S(2)}) copy-start(f32[1024,1024]{0,1:T(8,128)} %copy-done.35) | copy-start | bytes 12582916
  777.3 18.1 %copy-start.59 = (f32[1024,1024]{0,1:T(8,128)S(1)}, f32[1024,1024]{0,1:T(8,128)}, u32[]{:S(2)}) copy-start(f32[1024,1024]{0,1:T(8,128)} %fusion.130) | copy-start | bytes 12582916
  808.7 15.3 %copy-start.11 = (bf16[1024,16,64]{0,2,1:T(8,128)(2,1)S(1)}, bf16[1024,16,64]{0,2,1:T(8,128)(2,1)}, u32[]{:S(2)}) copy-start(bf16[1024,16,64]{0,2,1:T(8,128)(2,1)} %get-tuple-element.1408) | copy-start | bytes 6291460 | tf_op jit(solution)/shard_map/while/body/eval_jaxpr/while
  808.7 15.3 %copy-start.38 = (bf16[1024,16,64]{0,2,1:T(8,128)(2,1)S(1)}, bf16[1024,16,64]{0,2,1:T(8,128)(2,1)}, u32[]{:S(2)}) copy-start(bf16[1024,16,64]{0,2,1:T(8,128)(2,1)} %get-tuple-element.1407) | copy-start | bytes 6291460 | tf_op jit(solution)/shard_map/while/body/eval_jaxpr/while
  916.9 15.3 %copy-start.11 = (bf16[1024,16,64]{0,2,1:T(8,128)(2,1)S(1)}, bf16[1024,16,64]{0,2,1:T(8,128)(2,1)}, u32[]{:S(2)}) copy-start(bf16[1024,16,64]{0,2,1:T(8,128)(2,1)} %get-tuple-element.1408) | copy-start | bytes 6291460 | tf_op jit(solution)/shard_map/while/body/eval_jaxpr/while
  916.9 15.3 %copy-start.38 = (bf16[1024,16,64]{0,2,1:T(8,128)(2,1)S(1)}, bf16[1024,16,64]{0,2,1:T(8,128)(2,1)}, u32[]{:S(2)}) copy-start(bf16[1024,16,64]{0,2,1:T(8,128)(2,1)} %get-tuple-element.1407) | copy-start | bytes 6291460 | tf_op jit(solution)/shard_map/while/body/eval_jaxpr/while
  1047.8 15.3 %copy-start.8 = (bf16[1024,16,64]{0,2,1:T(8,128)(2,1)S(1)}, bf16[1024,16,64]{0,2,1:T(8,128)(2,1)}, u32[]{:S(2)}) copy-start(bf16[1024,16,64]{0,2,1:T(8,128)(2,1)} %get-tuple-element.1363) | copy-start | bytes 6291460 | tf_op jit(solution)/shard_map/while/body/eval_jaxpr/while
  1047.8 15.3 %copy-start.37 = (bf16[1024,16,64]{0,2,1:T(8,128)(2,1)S(1)}, bf16[1024,16,64]{0,2,1:T(8,128)(2,1)}, u32[]{:S(2)}) copy-start(bf16[1024,16,64]{0,2,1:T(8,128)(2,1)} %get-tuple-element.1362) | copy-start | bytes 6291460 | tf_op jit(solution)/shard_map/while/body/eval_jaxpr/while
  1156.0 15.3 %copy-start.8 = (bf16[1024,16,64]{0,2,1:T(8,128)(2,1)S(1)}, bf16[1024,16,64]{0,2,1:T(8,128)(2,1)}, u32[]{:S(2)}) copy-start(bf16[1024,16,64]{0,2,1:T(8,128)(2,1)} %get-tuple-element.1363) | copy-start | bytes 6291460 | tf_op jit(solution)/shard_map/while/body/eval_jaxpr/while
  1156.0 15.3 %copy-start.37 = (bf16[1024,16,64]{0,2,1:T(8,128)(2,1)S(1)}, bf16[1024,16,64]{0,2,1:T(8,128)(2,1)}, u32[]{:S(2)}) copy-start(bf16[1024,16,64]{0,2,1:T(8,128)(2,1)} %get-tuple-element.1362) | copy-start | bytes 6291460 | tf_op jit(solution)/shard_map/while/body/eval_jaxpr/while
  1291.5 11.2 copy-start.14
  1291.5 11.2 copy-start.28
  1291.5 11.2 copy-start.75
  1317.6 31.5 %copy-start.124 = (f32[1024]{0:T(1024)S(1)}, f32[1024]{0:T(1024)}, u32[]{:S(2)}) copy-start(f32[1024]{0:T(1024)} %copy-done.123) | copy-start | bytes 12292
  1317.6 31.5 %copy-start.134 = (f32[1024]{0:T(1024)S(1)}, f32[1024]{0:T(1024)}, u32[]{:S(2)}) copy-start(f32[1024]{0:T(1024)} %add_rsqrt_fusion.1) | copy-start | bytes 12292
  (110 other events, 431.4 us)
Sparse Core Ops, SparseCore 0:
  9.7 67.6 all-gather.5
  78.9 27.6 all-gather.7
  108.3 81.5 all-gather.11
  191.3 80.5 all-gather.9
  1385.3 117.5 all-reduce.2
where the time goes:
time: 1520 us
  matrix products  838 us (55%)
  other arithmetic  373 us (25%)
  local copies, waits for them, and re-layouts  136 us (9%)
  waiting for transfers between devices  104 us (7%)
  blocking collectives  38.4 us (3%)
  between operations  15.6 us (1%)
    dot_general x12, matrix products, one_block(): jnp.einsum('qhd,khd->hqk', query_block, key_rows, preferred_element_type=...  186 us
    sub x4, other arithmetic, one_block(): exponent = jnp.exp(masked - highest)  155 us
    dot_general x8, matrix products, one_block(): jnp.einsum('hqk,khd->qhd', prob_low, value_vectors, preferred_element_typ...  117 us
    convert_element_type x4, other arithmetic, one_block(): grad_scores = (probs * (grad_probs - row_delta)).astype(jnp.bfloat16)  111 us
    dot_general x4, matrix products, one_block(): jnp.einsum('qhd,khd->hqk', grad_block, value_vectors, preferred_element_t...  102 us
    psum x1, waiting for transfers between devices, per_device(): running_offset = lax.psum(running_offset, ('dp', 'fsdp'))  101 us
    dot_general x4, matrix products, one_block(): jnp.einsum('hqk,qhd->khd', prob_low, grad_block, preferred_element_type=j...  72.4 us
    unnamed x279, local copies, waits for them, and re-layouts  63.8 us
  transfers between devices with their start and end apart: 5, of which 1 were waited for; matrix products, arithmetic and copies ran while one was open for 43% of the time, Pallas kernels for 0%

commit v1 on v0

v1 whole, which is shorter than its diff:
```python
import functools
import math

import jax
import jax.numpy as jnp
from jax import lax
from jax.experimental import pallas as pl
from jax.experimental.pallas import tpu as pltpu
from jax.sharding import PartitionSpec as P

f32 = jnp.float32
bf16 = jnp.bfloat16
LANES = 128
PAIR = 128
BAND = 3
EPS = 1e-5
MASKED = -1e30
SCORE_SCALE = 0.125 * math.log2(math.e)
GELU_C = math.sqrt(2.0 / math.pi)
VMEM_LIMIT = 58 * 2**20
NT = (((1,), (1,)), ((), ()))
TN = (((0,), (0,)), ((), ()))


def dot(a, b):
    return jnp.dot(a, b, preferred_element_type=f32)


def dot_nt(a, b):
    return lax.dot_general(a, b, NT, preferred_element_type=f32)


def dot_tn(a, b):
    return lax.dot_general(a, b, TN, preferred_element_type=f32)


def params():
    return pltpu.CompilerParams(vmem_limit_bytes=VMEM_LIMIT)


def resident(array):
    zeros = (0,) * array.ndim
    return pl.BlockSpec(array.shape, lambda *_: zeros, pipeline_mode=pl.Buffered(1))


def normalise(x):
    centred = x - jnp.mean(x, axis=-1, keepdims=True)
    r = lax.rsqrt(jnp.mean(centred * centred, axis=-1, keepdims=True) + EPS)
    return centred * r, r


def norm_back(n, r, w):
    return r * (w - jnp.mean(w, axis=-1, keepdims=True) - n * jnp.mean(w * n, axis=-1, keepdims=True))


def gelu_and_slope(x):
    x2 = x * x
    t = jnp.tanh(x * (GELU_C + (GELU_C * 0.044715) * x2))
    half = 0.5 + 0.5 * t
    slope = half + (0.5 * x) * ((1.0 - t * t) * (GELU_C + (3 * GELU_C * 0.044715) * x2))
    return x * half, slope


def project_kernel(tok, w, down, up, vec, q_ref, k_ref, v_ref, low_ref):
    width = tok.shape[1]
    n, _ = normalise(tok[...].astype(f32))
    normed = (n * vec[6:7, :] + vec[0:1, :]).astype(bf16)
    low = dot(normed, down[...]).astype(bf16)
    low_ref[...] = low
    q = dot(normed, w[:, :width]) + dot(low, up[:, :width]) + vec[2:3, :]
    q_ref[...] = (q * SCORE_SCALE).astype(bf16)
    k_ref[...] = dot(normed, w[:, width : 2 * width]).astype(bf16)
    v = dot(normed, w[:, 2 * width :]) + dot(low, up[:, width:]) + vec[3:4, :]
    v_ref[...] = v.astype(bf16)


def project(tok, w, down, up, vec):
    tokens, width = tok.shape
    rows = 512
    row = pl.BlockSpec((rows, width), lambda i: (i, 0))
    return pl.pallas_call(
        project_kernel,
        grid=(tokens // rows,),
        in_specs=[row, resident(w), resident(down), resident(up), resident(vec)],
        out_specs=[row] * 3 + [pl.BlockSpec((rows, LANES), lambda i: (i, 0))],
        out_shape=[jax.ShapeDtypeStruct((tokens, width), bf16)] * 3
        + [jax.ShapeDtypeStruct((tokens, LANES), bf16)],
        compiler_params=params(),
        name="project",
    )(tok, w, down, up, vec)


def document_of(place, starts):
    number = jnp.zeros(place.shape, jnp.int32)
    for start in starts:
        number = number + (place >= start).astype(jnp.int32)
    return number


def fill_masks(lengths, slot, mask, blocks):
    starts = []
    total = jnp.int32(0)
    for d in range(lengths.shape[1]):
        starts.append(total)
        total = total + lengths[slot, d]
    for qb in range(blocks):
        first = max(0, qb - BAND + 1)
        rows = (qb - first + 1) * LANES
        key = first * LANES + lax.broadcasted_iota(jnp.int32, (rows, LANES), 0)
        query = qb * LANES + lax.broadcasted_iota(jnp.int32, (rows, LANES), 1)
        ok = (document_of(key, starts) == document_of(query, starts)) & (key <= query)
        mask[qb, :rows, :] = jnp.where(ok, 0.0, MASKED)


def half_lanes():
    return lax.broadcasted_iota(jnp.int32, (LANES, LANES), 1) < 64


def half_rows():
    return lax.broadcasted_iota(jnp.int32, (LANES, LANES), 0) < 64


def split_heads(x, left):
    zero = jnp.zeros_like(x)
    return jnp.concatenate([jnp.where(left, x, zero), jnp.where(left, zero, x)], axis=0)


def pipelined(units, stages, lags):
    for t in range(len(units) + lags[-1]):
        for stage, lag in zip(stages, lags):
            if 0 <= t - lag < len(units):
                stage(units[t - lag])


def geometry(qb):
    first = max(0, qb - BAND + 1)
    return first * LANES, (qb - first + 1) * LANES


def attend_kernel(pairs, blocks, lengths, q_ref, k_ref, v_ref, o_ref, p_ref, linv_ref, mask):
    @pl.when(pl.program_id(1) == 0)
    def _():
        fill_masks(lengths, pl.program_id(0), mask, blocks)

    left, top = half_lanes(), half_rows()
    scores, probs = {}, {}

    def score(unit):
        pair, qb = unit
        cols = slice(pair * PAIR, (pair + 1) * PAIR)
        key0, rows = geometry(qb)
        q = split_heads(q_ref[qb * LANES : (qb + 1) * LANES, cols], left)
        scores[unit] = dot_nt(k_ref[key0 : key0 + rows, cols], q)

    def soften(unit):
        pair, qb = unit
        key0, rows = geometry(qb)
        bias = mask[qb, :rows, :]
        s = scores.pop(unit) + jnp.concatenate([bias, bias], axis=1)
        p = jnp.exp2(s - jnp.max(s, axis=0, keepdims=True))
        linv = 1.0 / jnp.sum(p, axis=0, keepdims=True)
        linv_ref[0, pair, qb : qb + 1, :] = linv
        low = p.astype(bf16)
        p_ref[0, pair, qb, :rows, :] = low
        probs[unit] = (low, linv)

    def mix(unit):
        pair, qb = unit
        cols = slice(pair * PAIR, (pair + 1) * PAIR)
        key0, rows = geometry(qb)
        low, linv = probs.pop(unit)
        o = dot_tn(v_ref[key0 : key0 + rows, cols], low)
        o = jnp.where(top, o[:, :LANES] * linv[:, :LANES], o[:, LANES:] * linv[:, LANES:])
        o_ref[qb * LANES : (qb + 1) * LANES, cols] = o.T.astype(bf16)

    units = [(pair, qb) for qb in range(blocks) for pair in range(pairs)]
    pipelined(units, (score, soften, mix), (0, 2, 5))


def attend(lengths, q, k, v):
    slots = lengths.shape[0]
    tokens, width = q.shape
    seq = tokens // slots
    blocks, heads2, pairs = seq // LANES, width // PAIR, 2
    rows = BAND * LANES
    tile = pl.BlockSpec((seq, pairs * PAIR), lambda s, h, _: (s, h))
    return pl.pallas_call(
        functools.partial(attend_kernel, pairs, blocks),
        grid_spec=pltpu.PrefetchScalarGridSpec(
            num_scalar_prefetch=1,
            grid=(slots, heads2 // pairs),
            in_specs=[tile] * 3,
            out_specs=[
                tile,
                pl.BlockSpec((1, pairs, blocks, rows, 2 * LANES), lambda s, h, _: (s, h, 0, 0, 0)),
                pl.BlockSpec((1, pairs, blocks, 2 * LANES), lambda s, h, _: (s, h, 0, 0)),
            ],
            scratch_shapes=[pltpu.VMEM((blocks, rows, LANES), f32)],
        ),
        out_shape=[
            jax.ShapeDtypeStruct(q.shape, bf16),
            jax.ShapeDtypeStruct((slots, heads2, blocks, rows, 2 * LANES), bf16),
            jax.ShapeDtypeStruct((slots, heads2, blocks, 2 * LANES), f32),
        ],
        compiler_params=params(),
        name="attend",
    )(lengths, q, k, v)


def attend_back_kernel(
    pairs, blocks, q_ref, k_ref, v_ref, g_ref, o_ref, p_ref, linv_ref, dq_ref, dk_ref, dv_ref, dk_sum, dv_sum
):
    left, top = half_lanes(), half_rows()
    ones = jnp.ones((BAND * LANES, LANES), bf16)
    dk_sum[...] = jnp.zeros_like(dk_sum)
    dv_sum[...] = jnp.zeros_like(dv_sum)
    first, second = {}, {}

    def grad_probs(unit):
        pair, qb = unit
        cols = slice(pair * PAIR, (pair + 1) * PAIR)
        key0, rows = geometry(qb)
        here = slice(qb * LANES, (qb + 1) * LANES)
        linv = linv_ref[0, pair, qb : qb + 1, :]
        linv = jnp.where(top, linv[:, :LANES], linv[:, LANES:]).T
        g = g_ref[here, cols].astype(f32) * linv
        delta = split_heads(-(g * o_ref[here, cols].astype(f32)).astype(bf16), left)
        g = split_heads(g.astype(bf16), left)
        values = jnp.concatenate([v_ref[key0 : key0 + rows, cols], ones[:rows]], axis=1)
        first[unit] = (dot_nt(values, jnp.concatenate([g, delta], axis=1)), g)

    def grad_values(unit):
        pair, qb = unit
        cols = slice(pair * PAIR, (pair + 1) * PAIR)
        key0, rows = geometry(qb)
        dp, g = first.pop(unit)
        low = p_ref[0, pair, qb, :rows, :]
        second[unit] = low * dp.astype(bf16)
        dv_sum[key0 : key0 + rows, cols] += dot(low, g)

    def grad_queries_keys(unit):
        pair, qb = unit
        cols = slice(pair * PAIR, (pair + 1) * PAIR)
        key0, rows = geometry(qb)
        here = slice(qb * LANES, (qb + 1) * LANES)
        ds = second.pop(unit)
        dk_sum[key0 : key0 + rows, cols] += dot(ds, split_heads(q_ref[here, cols], left))
        dq = dot_tn(k_ref[key0 : key0 + rows, cols], ds)
        dq = jnp.where(top, dq[:, :LANES], dq[:, LANES:]) * 0.125
        dq_ref[here, cols] = dq.T.astype(bf16)

    units = [(pair, qb) for qb in range(blocks) for pair in range(pairs)]
    pipelined(units, (grad_probs, grad_values, grad_queries_keys), (0, 2, 4))
    dk_ref[...] = (dk_sum[...] * (0.125 / SCORE_SCALE)).astype(bf16)
    dv_ref[...] = dv_sum[...].astype(bf16)


def attend_back(slots, q, k, v, g, o, p, linv):
    tokens, width = q.shape
    seq = tokens // slots
    blocks, heads2, pairs = seq // LANES, width // PAIR, 2
    rows = BAND * LANES
    tile = pl.BlockSpec((seq, pairs * PAIR), lambda s, h: (s, h))
    return pl.pallas_call(
        functools.partial(attend_back_kernel, pairs, blocks),
        grid=(slots, heads2 // pairs),
        in_specs=[tile] * 5
        + [
            pl.BlockSpec((1, pairs, blocks, rows, 2 * LANES), lambda s, h: (s, h, 0, 0, 0)),
            pl.BlockSpec((1, pairs, blocks, 2 * LANES), lambda s, h: (s, h, 0, 0)),
        ],
        out_specs=[tile] * 3,
        scratch_shapes=[pltpu.VMEM((seq, pairs * PAIR), f32)] * 2,
        out_shape=[jax.ShapeDtypeStruct(q.shape, bf16)] * 3,
        compiler_params=params(),
        name="attend_back",
    )(q, k, v, g, o, p, linv)


def feed_chunk(normed, cot, up, down, bias):
    act, slope = gelu_and_slope(dot(normed, up) + bias)
    grad = slope * dot_nt(cot, down)
    return dot(act.astype(bf16), down), dot_nt(grad.astype(bf16), up)


def feed_first_kernel(tok, att, cot, wo, up, down, vec, bias, h1_ref, normed_ref, sum_o, sum_g):
    h1 = tok[...].astype(f32) + dot(att[...], wo[...]) + vec[4:5, :]
    h1_ref[...] = h1
    n, _ = normalise(h1)
    normed = (n * vec[7:8, :] + vec[1:2, :]).astype(bf16)
    normed_ref[...] = normed
    sum_o[...], sum_g[...] = feed_chunk(normed, cot[...], up[...], down[...], bias[...])


def feed_middle_kernel(normed, cot, old_o, old_g, up, down, bias, sum_o, sum_g):
    o, g = feed_chunk(normed[...], cot[...], up[...], down[...], bias[...])
    sum_o[...] = old_o[...] + o
    sum_g[...] = old_g[...] + g


def feed_last_kernel(h1, normed, cot, old_o, old_g, wo, up, down, vec, bias, out_ref, gh_ref, ga_ref):
    o, g = feed_chunk(normed[...], cot[...], up[...], down[...], bias[...])
    x = h1[...]
    out_ref[...] = (x + (old_o[...] + o) + vec[5:6, :]).astype(bf16)
    n, r = normalise(x)
    grad = cot[...].astype(f32) + norm_back(n, r, (old_g[...] + g) * vec[7:8, :])
    low = grad.astype(bf16)
    gh_ref[...] = low
    ga_ref[...] = dot_nt(low, wo[...]).astype(bf16)


def feed_call(kernel, name, rowwise, shared, out_types):
    tokens, width = rowwise[0].shape
    rows = 512
    row = pl.BlockSpec((rows, width), lambda i: (i, 0))
    return pl.pallas_call(
        kernel,
        grid=(tokens // rows,),
        in_specs=[row] * len(rowwise) + [resident(a) for a in shared],
        out_specs=[row] * len(out_types),
        out_shape=[jax.ShapeDtypeStruct((tokens, width), t) for t in out_types],
        compiler_params=params(),
        name=name,
    )(*rowwise, *shared)


def adapter_kernel(tok, dq, dv, low, up, vec, glow_ref, grads):
    width = tok.shape[1]
    n, _ = normalise(tok[...].astype(f32))
    normed = (n * vec[6:7, :] + vec[0:1, :]).astype(bf16)
    glow = (dot_nt(dq[...], up[:, :width]) + dot_nt(dv[...], up[:, width:])).astype(bf16)
    glow_ref[...] = glow
    part = jnp.concatenate(
        [
            dot_tn(low[...], dq[...])[0:4] * 8.0,
            dot_tn(low[...], dv[...])[4:8] * 8.0,
            dot_tn(glow, normed)[0:8],
        ],
        axis=0,
    )

    @pl.when(pl.program_id(0) == 0)
    def _():
        grads[...] = part

    @pl.when(pl.program_id(0) != 0)
    def _():
        grads[...] += part


def adapter_grads(tok, dq, dv, low, up, vec):
    tokens, width = tok.shape
    rows = 1024
    row = pl.BlockSpec((rows, width), lambda i: (i, 0))
    thin = pl.BlockSpec((rows, LANES), lambda i: (i, 0))
    return pl.pallas_call(
        adapter_kernel,
        grid=(tokens // rows,),
        in_specs=[row, row, row, thin, resident(up), resident(vec)],
        out_specs=[thin, pl.BlockSpec((16, width), lambda i: (0, 0))],
        out_shape=[jax.ShapeDtypeStruct((tokens, LANES), bf16), jax.ShapeDtypeStruct((16, width), f32)],
        compiler_params=params(),
        name="adapter_grads",
    )(tok, dq, dv, low, up, vec)


def input_kernel(tok, gh, dq, dk, dv, glow, w, down, vec, out_ref):
    width = tok.shape[1]
    g = dot_nt(dq[...], w[:, :width])
    g = g + dot_nt(dk[...], w[:, width : 2 * width])
    g = g + dot_nt(dv[...], w[:, 2 * width :])
    g = g + dot_nt(glow[...], down[...])
    n, r = normalise(tok[...].astype(f32))
    out_ref[...] = (gh[...].astype(f32) + norm_back(n, r, g * vec[6:7, :])).astype(bf16)


def input_grad(tok, gh, dq, dk, dv, glow, w, down, vec):
    tokens, width = tok.shape
    rows = 512
    row = pl.BlockSpec((rows, width), lambda i: (i, 0))
    thin = pl.BlockSpec((rows, LANES), lambda i: (i, 0))
    return pl.pallas_call(
        input_kernel,
        grid=(tokens // rows,),
        in_specs=[row] * 5 + [thin, resident(w), resident(down), resident(vec)],
        out_specs=row,
        out_shape=jax.ShapeDtypeStruct((tokens, width), bf16),
        compiler_params=params(),
        name="input_grad",
    )(tok, gh, dq, dk, dv, glow, w, down, vec)


def per_device(
    tokens,
    document_length_list,
    joint_projection_weight,
    attention_out_weight,
    feed_up_weight,
    feed_down_weight,
    frozen_norm_gains,
    biases,
    hidden_up_bias,
    query_down_adapter,
    query_up_adapter,
    value_down_adapter,
    value_up_adapter,
    cotangent,
):
    micro, local, seq, width = tokens.shape
    slots = micro * local
    shards = width // joint_projection_weight.shape[0]
    hidden = feed_down_weight.shape[0]
    tok = tokens.reshape(slots * seq, width)
    cot = cotangent.reshape(slots * seq, width)
    lengths = document_length_list.reshape(slots, -1)

    small = jnp.concatenate([biases, frozen_norm_gains], axis=0)
    small = jnp.concatenate([small.reshape(-1), hidden_up_bias])
    small = lax.all_gather(small, "fsdp", axis=0, tiled=False).astype(f32)
    head = small.shape[1] - hidden
    vec = small[:, :head].reshape(shards, 8, width // shards).transpose(1, 0, 2).reshape(8, width)
    hidden_bias = small[:, head:]

    joint = lax.all_gather(joint_projection_weight, "fsdp", axis=0, tiled=True)
    wo = lax.all_gather(attention_out_weight, "fsdp", axis=0, tiled=True)

    chunks = 4
    part = hidden // chunks
    up_parts = feed_up_weight.reshape(-1, shards, chunks, part)
    feeds = []
    for j in range(chunks):
        up = up_parts[:, :, j, :].reshape(-1, shards * part)
        down = feed_down_weight[j * part : (j + 1) * part]
        up = lax.all_gather(up, "fsdp", axis=0, tiled=True)
        down = lax.all_gather(down, "fsdp", axis=0, tiled=True)
        bias = hidden_bias[:, j * part : (j + 1) * part].reshape(1, -1)
        feeds.append((up, down, bias))

    rank = query_down_adapter.shape[1]
    down_map = jnp.concatenate([query_down_adapter, value_down_adapter], axis=1)
    down_map = jnp.pad(down_map, ((0, 0), (0, LANES - 2 * rank)))
    zero = jnp.zeros_like(query_up_adapter)
    up_map = jnp.concatenate(
        [
            jnp.concatenate([query_up_adapter, zero], axis=1),
            jnp.concatenate([zero, value_up_adapter], axis=1),
        ],
        axis=0,
    )
    up_map = jnp.pad(up_map * 8, ((0, LANES - 2 * rank), (0, 0))).astype(bf16)

    q, k, v, low = project(tok, joint, down_map, up_map, vec)
    att, probs, linv = attend(lengths, q, k, v)

    up, down, bias = feeds[0]
    h1, normed, sum_o, sum_g = feed_call(
        feed_first_kernel, "feed_first", [tok, att, cot], [wo, up, down, vec, bias], [f32, bf16, f32, f32]
    )
    for up, down, bias in feeds[1:-1]:
        sum_o, sum_g = feed_call(
            feed_middle_kernel, "feed_middle", [normed, cot, sum_o, sum_g], [up, down, bias], [f32, f32]
        )
    up, down, bias = feeds[-1]
    out, gh, ga = feed_call(
        feed_last_kernel,
        "feed_last",
        [h1, normed, cot, sum_o, sum_g],
        [wo, up, down, vec, bias],
        [bf16, bf16, bf16],
    )

    dq, dk, dv = attend_back(slots, q, k, v, ga, att, probs, linv)
    glow, grads = adapter_grads(tok, dq, dv, low, up_map, vec)
    grads = lax.all_gather(grads, ("dp", "fsdp"), axis=0, tiled=False)
    grad_in = input_grad(tok, gh, dq, dk, dv, glow, joint, down_map, vec)
    grads = jnp.sum(grads, axis=0)
    return (
        out.reshape(tokens.shape),
        grad_in.reshape(tokens.shape),
        grads[8:12].T,
        grads[0:4],
        grads[12:16].T,
        grads[4:8],
    )


def solution(mesh):
    slots = P(None, ("dp", "fsdp"), None, None)
    return jax.shard_map(
        per_device,
        mesh=mesh,
        in_specs=(
            slots,
            P(None, ("dp", "fsdp"), None),
            P("fsdp", None),
            P("fsdp", None),
            P("fsdp", None),
            P("fsdp", None),
            P(None, "fsdp"),
            P(None, "fsdp"),
            P("fsdp"),
            P(),
            P(),
            P(),
            P(),
            slots,
        ),
        out_specs=(slots, slots, P(), P(), P(), P()),
        check_vma=False,
    )
```

time: 1520 us -> 491 us (0.32)
  matrix products: 838 us -> 0 us
  other arithmetic: 373 us -> 1.75 us
  Pallas kernels: 0 us -> 228 us
  local copies, waits for them, and re-layouts: 136 us -> 15.4 us
  waiting for transfers between devices: 104 us -> 211 us
  blocking collectives: 38.4 us -> 16.6 us
    dot_general x78 -> x0, matrix products: 838 us -> none  [the longest x12 186 us: one_block(): jnp.einsum('qhd,khd->hqk', query_block, key_rows, preferred_element_type=...]
    pallas_call x0 -> x9, Pallas kernels: none -> 228 us  [the longest x4 114 us: feed_call(): pl.pallas_call(kernel, grid=(tokens // rows,), in_specs=[row] * len(rowwi...]
    all_gather x4 -> x11, waiting for transfers between devices: 0.01 us -> 207 us  [the longest x4 119 us: per_device(): down = lax.all_gather(down, 'fsdp', axis=0, tiled=True)]
    sub x5 -> x0, other arithmetic: 155 us -> none  [the longest x4 155 us: one_block(): exponent = jnp.exp(masked - highest)]
    convert_element_type x6 -> x0, other arithmetic: 114 us -> none  [the longest x4 111 us: one_block(): grad_scores = (probs * (grad_probs - row_delta)).astype(jnp.bfloat16)]
    psum x1 -> x0, waiting for transfers between devices: 101 us -> none  [per_device(): running_offset = lax.psum(running_offset, ('dp', 'fsdp'))]
    reduce_sum x16 -> x1, other arithmetic: 76.9 us -> 1.7 us  [per_device(): grads = jnp.sum(grads, axis=0)]
    unnamed x279 -> x22, local copies, waits for them, and re-layouts: 63.8 us -> 3.07 us
  transfers between devices with their start and end apart: 5 -> 11, of which waited for: 1 -> 9; matrix products, arithmetic and copies ran while one was open for 43% -> 3% of each run, Pallas kernels for 0% -> 32%
where the time goes in v1:
time: 491 us; the launch traced here: 487 us
  Pallas kernels  228 us (46%)
  waiting for transfers between devices  211 us (43%)
  blocking collectives  16.6 us (3%)
  local copies, waits for them, and re-layouts  15.4 us (3%)
  between operations  14.3 us (3%)
    all_gather x4, waiting for transfers between devices, per_device(): down = lax.all_gather(down, 'fsdp', axis=0, tiled=True)  119 us
    pallas_call x4, Pallas kernels, feed_call(): pl.pallas_call(kernel, grid=(tokens // rows,), in_specs=[row] * len(rowwi...  114 us
    all_gather x1, waiting for transfers between devices, per_device(): joint = lax.all_gather(joint_projection_weight, 'fsdp', axis=0, tiled=True)  34.9 us
    all_gather x1, waiting for transfers between devices, per_device(): grads = lax.all_gather(grads, ('dp', 'fsdp'), axis=0, tiled=False)  31.6 us
    pallas_call x1, Pallas kernels, attend_back(): pl.pallas_call(functools.partial(attend_back_kernel, pairs, blocks), grid...  28.8 us
    pallas_call x1, Pallas kernels, project(): pl.pallas_call(project_kernel, grid=(tokens // rows,), in_specs=[row, res...  25.3 us
    pallas_call x1, Pallas kernels, input_grad(): pl.pallas_call(input_kernel, grid=(tokens // rows,), in_specs=[row] * 5 +...  24.5 us
    pallas_call x1, Pallas kernels, attend(): pl.pallas_call(functools.partial(attend_kernel, pairs, blocks), grid_spec...  24.3 us
  transfers between devices with their start and end apart: 11, of which 9 were waited for; matrix products, arithmetic and copies ran while one was open for 3% of the time, Pallas kernels for 32%

profile of v1, /device:TPU:0, one launch (start us, length us, event | category | flops | bytes accessed | tf_op | source)
XLA Modules:
  0.0 487.1 jit_solution(11848911154350509380)
XLA Ops:
  7.2 0.7 all-gather.15.cloned.1.call-update
  7.9 0.0 all-gather.17.cloned.1.call-start
  8.0 0.7 all-gather.17.cloned.1.call-update
  8.7 0.0 all-gather.19.cloned.1.call-start
  8.7 1.8 reshape.57
  10.5 5.9 %slice_reduce_fusion = (bf16[128,8,128]{2,1,0:T(8,128)(2,1)S(1)}, bf16[128,8,128]{2,1,0:T(8,128)(2,1)S(1)}, bf16[128,8,128]{2,1,0:T(8,128)(2,1)S(1)}, bf16[128,8,128]{2,1,0:T(8,128)(2,1)S(1)}) fusion(bf16[128,8,4,128]{3,2,1,0:T(4,128)(2,1)S(1)} %reshape.57), kind=kLoop, calls=%fused_computation | loop fusion | bytes 2097152 | tf_op jit(solution)/shard_map/slice | solution.py:432
  16.5 0.8 copy.54
  17.3 0.0 all-gather.21.cloned.1.call-start
  17.3 1.0 fusion.4
  18.4 0.0 all-gather.23.cloned.1.call-start
  18.4 0.8 copy.53
  19.2 0.0 all-gather.25.cloned.1.call-start
  19.2 0.5 all-gather.25.cloned.1.call-update
  19.8 0.0 all-gather.27.cloned.1.call-start
  19.8 0.8 copy.52
  20.6 0.0 all-gather.29.cloned.1.call-start
  20.6 0.7 all-gather.29.cloned.1.call-update
  21.4 0.0 all-gather.31.cloned.1.call-start
  21.4 0.7 copy.51
  22.2 0.0 all-gather.33.cloned.1.call-start
  22.2 0.5 all-gather.33.cloned.1.call-update
  22.8 0.0 all-gather.35.cloned.1.call-start
  22.8 0.2 copy.28
  23.0 0.8 pad.10.down
  23.8 0.9 pad.11.up
  24.7 16.6 %all-gather.2 = bf16[8,1,1536]{2,1,0:T(2,128)(2,1)S(1)} all-gather(bf16[1,1,1536]{2,1,0:T(2,128)(2,1)S(1)} %reshape.67), channel_id=2, replica_groups=mesh['dp'=4,'fsdp'=8] {'fsdp'}, dimensions={0}, use_global_device_ids=true | all-gather | bytes 27648 | tf_op jit(solution)/shard_map/all_gather | solution.py:419
  41.4 0.6 copy.56
  42.0 0.6 fusion.6
  42.6 34.9 %all-gather.15.cloned.1.call-done.w = bf16[1024,3072]{1,0:T(8,128)(2,1)} async-done(((bf16[128,3072]{1,0:T(8,128)(2,1)}), bf16[1024,3072]{1,0:T(8,128)(2,1)}) %all-gather.15.cloned.1.call-update) | async-done | bytes 6291472 | tf_op jit(solution)/shard_map/all_gather | solution.py:424
  77.5 25.3 %project.1 = (bf16[2048,1024]{1,0:T(8,128)(2,1)}, bf16[2048,1024]{1,0:T(8,128)(2,1)}, bf16[2048,1024]{1,0:T(8,128)(2,1)}, bf16[2048,128]{1,0:T(8,128)(2,1)}) custom-call(bf16[2048,1024]{1,0:T(8,128)(2,1)} %bitcast.46, bf16[1024,3072]{1,0:T(8,128)(2,1)} %all-gather.15.cloned.1.call-done.w, bf16[1024,128]{1,0:T(8,128)(2,1)} %pad.10.down, ...), custom_call_target="tpu_custom_call" | custom-call | tf_op jit(solution)/shard_map/project/pallas_call | solution.py:81
  102.7 24.3 %attend.1 = (bf16[2048,1024]{1,0:T(8,128)(2,1)}, bf16[2,8,8,384,256]{4,3,2,1,0:T(8,128)(2,1)}, f32[2,8,8,256]{3,2,1,0:T(8,128)}) custom-call(s32[2,8]{1,0:T(2,128)} %bitcast.75, bf16[2048,1024]{1,0:T(8,128)(2,1)} %get-tuple-element.29.q_ref, bf16[2048,1024]{1,0:T(8,128)(2,1)} %get-tuple-element.30.k_ref, bf16[2048,1024]{1,0:T(8,128)(2,1)} %get-tuple-element.31.v_ref), custom_call_target="tpu_custom_call" | custom-call | tf_op jit(solution)/shard_map/attend/pallas_call | solution.py:187
  127.1 10.6 %all-gather.19.cloned.1.call-done.up = bf16[1024,1024]{1,0:T(8,128)(2,1)} async-done(((bf16[128,1024]{1,0:T(8,128)(2,1)}), bf16[1024,1024]{1,0:T(8,128)(2,1)}) %all-gather.19.cloned.1.call-update) | async-done | bytes 2097168 | tf_op jit(solution)/shard_map/all_gather | solution.py:434
  137.6 30.1 %all-gather.21.cloned.1.call-done.down = bf16[1024,1024]{1,0:T(8,128)(2,1)} async-done(((bf16[128,1024]{1,0:T(8,128)(2,1)}), bf16[1024,1024]{1,0:T(8,128)(2,1)}) %all-gather.21.cloned.1.call-update) | async-done | bytes 2097168 | tf_op jit(solution)/shard_map/all_gather | solution.py:435
  167.7 31.1 %feed_first.1 = (f32[2048,1024]{1,0:T(8,128)}, bf16[2048,1024]{1,0:T(8,128)(2,1)}, f32[2048,1024]{1,0:T(8,128)}, f32[2048,1024]{1,0:T(8,128)}) custom-call(bf16[2048,1024]{1,0:T(8,128)(2,1)} %bitcast.47, bf16[2048,1024]{1,0:T(8,128)(2,1)} %get-tuple-element.32.att.o_ref, bf16[2048,1024]{1,0:T(8,128)(2,1)} %bitcast.50, ...), custom_call_target="tpu_custom_call" | custom-call | tf_op jit(solution)/shard_map/feed_first/pallas_call | solution.py:316
  198.8 29.1 %all-gather.25.cloned.1.call-done.down = bf16[1024,1024]{1,0:T(8,128)(2,1)} async-done(((bf16[128,1024]{1,0:T(8,128)(2,1)}), bf16[1024,1024]{1,0:T(8,128)(2,1)}) %all-gather.25.cloned.1.call-update) | async-done | bytes 2097168 | tf_op jit(solution)/shard_map/all_gather | solution.py:435
  227.9 24.7 %feed_middle.2 = (f32[2048,1024]{1,0:T(8,128)}, f32[2048,1024]{1,0:T(8,128)}) custom-call(bf16[2048,1024]{1,0:T(8,128)(2,1)} %get-tuple-element.34.normed, bf16[2048,1024]{1,0:T(8,128)(2,1)} %bitcast.51, f32[2048,1024]{1,0:T(8,128)} %get-tuple-element.35.old_o, f32[2048,1024]{1,0:T(8,128)} %get-tuple-element.36.old_g, ...), custom_call_target="tpu_custom_call" | custom-call | tf_op jit(solution)/shard_map/feed_middle/pallas_call | solution.py:316
  252.6 5.5 %all-gather.27.cloned.1.call-done.up = bf16[1024,1024]{1,0:T(8,128)(2,1)} async-done(((bf16[128,1024]{1,0:T(8,128)(2,1)}), bf16[1024,1024]{1,0:T(8,128)(2,1)}) %all-gather.27.cloned.1.call-update) | async-done | bytes 2097168 | tf_op jit(solution)/shard_map/all_gather | solution.py:434
  258.1 30.2 %all-gather.29.cloned.1.call-done.down = bf16[1024,1024]{1,0:T(8,128)(2,1)} async-done(((bf16[128,1024]{1,0:T(8,128)(2,1)}), bf16[1024,1024]{1,0:T(8,128)(2,1)}) %all-gather.29.cloned.1.call-update) | async-done | bytes 2097168 | tf_op jit(solution)/shard_map/all_gather | solution.py:435
  288.3 24.9 %feed_middle.3 = (f32[2048,1024]{1,0:T(8,128)}, f32[2048,1024]{1,0:T(8,128)}) custom-call(bf16[2048,1024]{1,0:T(8,128)(2,1)} %get-tuple-element.34.normed, bf16[2048,1024]{1,0:T(8,128)(2,1)} %bitcast.52, f32[2048,1024]{1,0:T(8,128)} %get-tuple-element.37.old_o, f32[2048,1024]{1,0:T(8,128)} %get-tuple-element.38.old_g, ...), custom_call_target="tpu_custom_call" | custom-call | tf_op jit(solution)/shard_map/feed_middle/pallas_call | solution.py:316
  313.3 5.3 %all-gather.31.cloned.1.call-done.up = bf16[1024,1024]{1,0:T(8,128)(2,1)} async-done(((bf16[128,1024]{1,0:T(8,128)(2,1)}), bf16[1024,1024]{1,0:T(8,128)(2,1)}) %all-gather.31.cloned.1.call-update) | async-done | bytes 2097168 | tf_op jit(solution)/shard_map/all_gather | solution.py:434
  318.6 30.1 %all-gather.33.cloned.1.call-done.down = bf16[1024,1024]{1,0:T(8,128)(2,1)} async-done(((bf16[128,1024]{1,0:T(8,128)(2,1)}), bf16[1024,1024]{1,0:T(8,128)(2,1)}) %all-gather.33.cloned.1.call-update) | async-done | bytes 2097168 | tf_op jit(solution)/shard_map/all_gather | solution.py:435
  348.7 33.6 %feed_last.1 = (bf16[2048,1024]{1,0:T(8,128)(2,1)}, bf16[2048,1024]{1,0:T(8,128)(2,1)}, bf16[2048,1024]{1,0:T(8,128)(2,1)}) custom-call(f32[2048,1024]{1,0:T(8,128)} %get-tuple-element.33.h1, bf16[2048,1024]{1,0:T(8,128)(2,1)} %get-tuple-element.34.normed, bf16[2048,1024]{1,0:T(8,128)(2,1)} %bitcast.53, f32[2048,1024]{1,0:T(8,128)} %get-tuple-element.39.old_o, ...), custom_call_target="tpu_custom_call" | custom-call | tf_op jit(solution)/shard_map/feed_last/pallas_call | solution.py:316
  382.3 28.8 %attend_back.1 = (bf16[2048,1024]{1,0:T(8,128)(2,1)}, bf16[2048,1024]{1,0:T(8,128)(2,1)}, bf16[2048,1024]{1,0:T(8,128)(2,1)}) custom-call(bf16[2048,1024]{1,0:T(8,128)(2,1)} %get-tuple-element.29.q_ref, bf16[2048,1024]{1,0:T(8,128)(2,1)} %get-tuple-element.30.k_ref, bf16[2048,1024]{1,0:T(8,128)(2,1)} %get-tuple-element.31.v_ref, ...), custom_call_target="tpu_custom_call" | custom-call | tf_op jit(solution)/shard_map/attend_back/pallas_call | solution.py:264
  411.1 10.8 %adapter_grads.1 = (bf16[2048,128]{1,0:T(8,128)(2,1)}, f32[16,1024]{1,0:T(8,128)}) custom-call(bf16[2048,1024]{1,0:T(8,128)(2,1)} %bitcast.48, bf16[2048,1024]{1,0:T(8,128)(2,1)} %get-tuple-element.46.dq, bf16[2048,1024]{1,0:T(8,128)(2,1)} %get-tuple-element.48.dv, bf16[2048,128]{1,0:T(8,128)(2,1)} %get-tuple-element.49.low, bf16[128,2048]{1,0:T(8,128)(2,1)} %pad.11.up, ...), custom_call_target="tpu_custom_call" | custom-call | tf_op jit(solution)/shard_map/adapter_grads/pallas_call | solution.py:356
  421.9 24.5 %input_grad.1 = bf16[2048,1024]{1,0:T(8,128)(2,1)} custom-call(bf16[2048,1024]{1,0:T(8,128)(2,1)} %bitcast.49, bf16[2048,1024]{1,0:T(8,128)(2,1)} %get-tuple-element.42.gh, bf16[2048,1024]{1,0:T(8,128)(2,1)} %get-tuple-element.46.dq, bf16[2048,1024]{1,0:T(8,128)(2,1)} %get-tuple-element.47.dk, bf16[2048,1024]{1,0:T(8,128)(2,1)} %get-tuple-element.48.dv, ...), custom_call_target="tpu_custom_call" | custom-call | tf_op jit(solution)/shard_map/input_grad/pallas_call | solution.py:382
  446.4 31.6 %all-gather.35.cloned.1.call-done = f32[512,1024]{1,0:T(8,128)} async-done(((f32[16,1024]{1,0:T(8,128)}), f32[512,1024]{1,0:T(8,128)}) %all-gather.35.cloned.1.call-update) | async-done | bytes 2097168 | tf_op jit(solution)/shard_map/all_gather | solution.py:474
  478.0 1.7 reduce_sum.9
  479.7 0.6 fusion.5
  (32 shorter events, 0.3 us)
Async XLA Ops:
  7.2 10.2 %copy-start = (bf16[512,1024]{1,0:T(8,128)(2,1)S(1)}, bf16[512,1024]{1,0:T(8,128)(2,1)}, u32[]{:S(2)}) copy-start(bf16[512,1024]{1,0:T(8,128)(2,1)} %param.19) | copy-start | bytes 3145732
  7.2 70.3 %all-gather.15.cloned.1.call-start = ((), (), s32[]{:S(2)}) async-start(), calls=%async_computation | async-start | bytes 7077888 | tf_op jit(solution)/shard_map/all_gather | solution.py:424
  7.9 119.2 %all-gather.17.cloned.1.call-start = ((), (), s32[]{:S(2)}) async-start(), calls=%async_computation.1 | async-start | bytes 2359296 | tf_op jit(solution)/shard_map/all_gather | solution.py:425
  8.7 129.0 %all-gather.19.cloned.1.call-start = ((), (), s32[]{:S(2)}) async-start(), calls=%async_computation.2 | async-start | bytes 2359296 | tf_op jit(solution)/shard_map/all_gather | solution.py:434
  10.5 12.3 %copy-start.1 = (bf16[1024,4]{0,1:T(4,128)(2,1)S(1)}, bf16[1024,4]{0,1:T(4,128)(2,1)}, u32[]{:S(2)}) copy-start(bf16[1024,4]{0,1:T(4,128)(2,1)} %param.25) | copy-start | bytes 24580
  10.5 12.3 %copy-start.2 = (bf16[1024,4]{0,1:T(4,128)(2,1)S(1)}, bf16[1024,4]{0,1:T(4,128)(2,1)}, u32[]{:S(2)}) copy-start(bf16[1024,4]{0,1:T(4,128)(2,1)} %param.23) | copy-start | bytes 24580
  16.4 7.3 %copy-start.3 = (bf16[4,1024]{1,0:T(4,128)(2,1)S(1)}, bf16[4,1024]{1,0:T(4,128)(2,1)}, u32[]{:S(2)}) copy-start(bf16[4,1024]{1,0:T(4,128)(2,1)} %param.26) | copy-start | bytes 24580
  16.5 7.3 %copy-start.4 = (bf16[4,1024]{1,0:T(4,128)(2,1)S(1)}, bf16[4,1024]{1,0:T(4,128)(2,1)}, u32[]{:S(2)}) copy-start(bf16[4,1024]{1,0:T(4,128)(2,1)} %param.24) | copy-start | bytes 24580
  16.5 8.2 %copy-start.5 = (bf16[6,128]{1,0:T(8,128)(2,1)S(1)}, bf16[6,128]{1,0:T(8,128)(2,1)}, u32[]{:S(2)}) copy-start(bf16[6,128]{1,0:T(8,128)(2,1)} %param.21) | copy-start | bytes 4612
  16.5 8.2 %copy-start.7 = (bf16[2,128]{1,0:T(2,128)(2,1)S(1)}, bf16[2,128]{1,0:T(2,128)(2,1)}, u32[]{:S(2)}) copy-start(bf16[2,128]{1,0:T(2,128)(2,1)} %param.20) | copy-start | bytes 1540
  16.5 8.2 %copy-start.6 = (bf16[512]{0:T(512)(128)(2,1)S(1)}, bf16[512]{0:T(512)(128)(2,1)}, u32[]{:S(2)}) copy-start(bf16[512]{0:T(512)(128)(2,1)} %param.22) | copy-start | bytes 3076
  17.3 150.4 %all-gather.21.cloned.1.call-start = ((), (), s32[]{:S(2)}) async-start(), calls=%async_computation.3 | async-start | bytes 2359296 | tf_op jit(solution)/shard_map/all_gather | solution.py:435
  18.4 180.4 %all-gather.23.cloned.1.call-start = ((), (), s32[]{:S(2)}) async-start(), calls=%async_computation.4 | async-start | bytes 2359296 | tf_op jit(solution)/shard_map/all_gather | solution.py:434
  19.2 208.7 %all-gather.25.cloned.1.call-start = ((), (), s32[]{:S(2)}) async-start(), calls=%async_computation.5 | async-start | bytes 2359296 | tf_op jit(solution)/shard_map/all_gather | solution.py:435
  19.8 238.3 %all-gather.27.cloned.1.call-start = ((), (), s32[]{:S(2)}) async-start(), calls=%async_computation.6 | async-start | bytes 2359296 | tf_op jit(solution)/shard_map/all_gather | solution.py:434
  20.6 267.7 %all-gather.29.cloned.1.call-start = ((), (), s32[]{:S(2)}) async-start(), calls=%async_computation.7 | async-start | bytes 2359296 | tf_op jit(solution)/shard_map/all_gather | solution.py:435
  21.4 297.2 %all-gather.31.cloned.1.call-start = ((), (), s32[]{:S(2)}) async-start(), calls=%async_computation.8 | async-start | bytes 2359296 | tf_op jit(solution)/shard_map/all_gather | solution.py:434
  22.2 326.5 %all-gather.33.cloned.1.call-start = ((), (), s32[]{:S(2)}) async-start(), calls=%async_computation.9 | async-start | bytes 2359296 | tf_op jit(solution)/shard_map/all_gather | solution.py:435
  22.8 455.2 %all-gather.35.cloned.1.call-start = ((), (), s32[]{:S(2)}) async-start(), calls=%async_computation.10 | async-start | bytes 2162688 | tf_op jit(solution)/shard_map/all_gather | solution.py:474
Sparse Core Ops, SparseCore 0:
  9.7 67.7 all-gather.14
  79.0 27.7 all-gather.16
  109.0 28.5 all-gather.18
  139.1 28.5 all-gather.20
  169.2 28.5 all-gather.22
  199.2 28.5 all-gather.24
  229.5 28.5 all-gather.26
  259.7 28.5 all-gather.28
  289.9 28.5 all-gather.30
  320.0 28.5 all-gather.32
  422.0 55.9 all-gather.34

commit v2 on v1

v2 whole, which is shorter than its diff:
```python
import functools
import math

import jax
import jax.numpy as jnp
from jax import lax
from jax.experimental import pallas as pl
from jax.experimental.pallas import tpu as pltpu
from jax.sharding import PartitionSpec as P

f32 = jnp.float32
bf16 = jnp.bfloat16
LANES = 128
PAIR = 128
BAND = 3
EPS = 1e-5
MASKED = -1e30
SCORE_SCALE = 0.125 * math.log2(math.e)
GELU_C = math.sqrt(2.0 / math.pi)
VMEM_LIMIT = 58 * 2**20
COST = 8
NT = (((1,), (1,)), ((), ()))
TN = (((0,), (0,)), ((), ()))


def dot(a, b):
    return jnp.dot(a, b, preferred_element_type=f32)


def dot_nt(a, b):
    return lax.dot_general(a, b, NT, preferred_element_type=f32)


def dot_tn(a, b):
    return lax.dot_general(a, b, TN, preferred_element_type=f32)


def params():
    return pltpu.CompilerParams(vmem_limit_bytes=VMEM_LIMIT)


def resident(array):
    zeros = (0,) * array.ndim
    return pl.BlockSpec(array.shape, lambda *_: zeros, pipeline_mode=pl.Buffered(1))


def normalise(x):
    centred = x - jnp.mean(x, axis=-1, keepdims=True)
    r = lax.rsqrt(jnp.mean(centred * centred, axis=-1, keepdims=True) + EPS)
    return centred * r, r


def norm_back(n, r, w):
    return r * (w - jnp.mean(w, axis=-1, keepdims=True) - n * jnp.mean(w * n, axis=-1, keepdims=True))


def gelu_and_slope(x):
    x2 = x * x
    t = jnp.tanh(x * (GELU_C + (GELU_C * 0.044715) * x2))
    half = 0.5 + 0.5 * t
    slope = half + (0.5 * x) * ((1.0 - t * t) * (GELU_C + (3 * GELU_C * 0.044715) * x2))
    return x * half, slope


def ring_pairs(dp, fsdp, move):
    pairs = []
    for d in range(dp):
        for f in range(fsdp):
            e, g = move(d, f)
            pairs.append((d * fsdp + f, e * fsdp + g))
    return pairs


def after(x, others):
    return lax.optimization_barrier((x, others))[0]


def after_all(xs, others):
    return lax.optimization_barrier((xs, others))[0]


class Gather:
    def __init__(self, dp, fsdp):
        self.dp, self.fsdp = dp, fsdp

    def move(self, x, where):
        return lax.ppermute(x, ("dp", "fsdp"), ring_pairs(self.dp, self.fsdp, where))

    def step_1(self, mine):
        fsdp = self.fsdp
        return [self.move(mine, lambda d, f, k=k: (d, (f + 2 * k) % fsdp)) for k in range(1, fsdp // 2)]

    def step_2(self, near):
        near = jnp.broadcast_to(near[None], (self.dp,) + near.shape)
        return lax.all_to_all(near, "dp", 0, 0, tiled=False)

    def step_3(self, far):
        return [far, self.swap(far)]

    def swap(self, x):
        return self.move(x, lambda d, f: (d, f ^ 1))


def copies(weight, refs, whole, sems, place, cols):
    made = []
    start, size = cols

    def add(source, first, at, rows):
        target = whole.at[pl.ds(at, rows), pl.ds(start, size)]
        made.append(pltpu.make_async_copy(source.at[:, pl.ds(first + start, size)], target, sems.at[len(made)]))

    if len(weight) == 1:
        add(refs[0], 0, 0, whole.shape[0])
        return made
    offset = weight[-1]
    index = place[1]
    rows = refs[0].shape[0]
    fsdp = whole.shape[0] // rows
    dp, near, _ = refs[2].shape
    part = near // (fsdp // 2 - 1)
    core = lax.rem(index, 2)
    for swapped in (0, 1):
        owner = index + swapped * (1 - 2 * core)
        add(refs[swapped], offset, pl.multiple_of(owner * rows, rows), rows)
        for e in range(dp):
            for k in range(1, fsdp // 2):
                owner = lax.rem(index + fsdp - 2 * k, fsdp) + swapped * (1 - 2 * core)
                at = pl.multiple_of(owner * rows + e * part, part)
                add(refs[2 + swapped].at[e, pl.ds((k - 1) * part, part)], 0, at, part)
    return made


def copy_count(weight, fsdp):
    return 1 if len(weight) == 1 else 2 + 2 * weight[2].shape[0] * (fsdp // 2 - 1)


def weight_call(kernel, name, weights, order, grid, blocked, in_specs, out_specs, out_shape, scratch, place, cost, fsdp, old=()):
    arrays = [w if len(w) == 1 else w[:-1] for w, _ in weights]
    flat = [a for some in arrays for a in some]
    counts = [copy_count(weights[i][0], fsdp) for i, _, _ in order]

    def body(place_ref, *refs):
        refs = list(refs)
        take = lambda n: [refs.pop(0) for _ in range(n)]
        sources = [take(len(some)) for some in arrays]
        ins, _, outs = take(len(blocked)), take(len(old)), take(len(out_shape))
        wholes, sems = take(len(weights)), take(len(order))

        first_step = pl.program_id(0) == 0
        for axis in range(1, len(grid)):
            first_step = first_step & (pl.program_id(axis) == 0)

        def group(n):
            i, start, size = order[n]
            return copies(weights[i][0], sources[i], wholes[i], sems[n], place_ref, (start, size))

        @pl.when(first_step)
        def _():
            for n in range(len(order)):
                for copy in group(n):
                    copy.start()

        def wait(n):
            @pl.when(first_step)
            def _():
                for copy in group(n):
                    copy.wait()

        kernel(wholes, wait, ins, outs, refs)

    return pl.pallas_call(
        body,
        grid_spec=pltpu.PrefetchScalarGridSpec(
            num_scalar_prefetch=1,
            grid=grid,
            in_specs=[pl.BlockSpec(memory_space=pl.ANY)] * len(flat)
            + in_specs
            + [pl.BlockSpec(memory_space=pl.ANY)] * len(old),
            out_specs=out_specs,
            scratch_shapes=[pltpu.VMEM(shape, bf16) for _, shape in weights]
            + [pltpu.SemaphoreType.DMA((n,)) for n in counts]
            + scratch,
        ),
        out_shape=out_shape,
        compiler_params=params(),
        cost_estimate=pl.CostEstimate(flops=cost // COST, bytes_accessed=2**20, transcendentals=0),
        input_output_aliases={1 + len(flat) + len(blocked) + i: i for i in range(len(old))},
        name=name,
    )(place, *flat, *blocked, *old)


def own_quarter(rows):
    return pl.ds(pl.multiple_of(lax.axis_index("dp") * rows, rows), rows)


def stack_rows(arrays, rows):
    arrays = [a.astype(f32) for a in arrays]
    used = sum(a.shape[0] for a in arrays)
    return jnp.concatenate(arrays + [jnp.zeros((rows - used, arrays[0].shape[1]), f32)], axis=0).astype(bf16)


def cut_kernel(joint, biases, gains, hidden, first, second, quarter):
    half = second.shape[1] // 3
    for i in range(3):
        first[:, i * half : (i + 1) * half] = joint[:, 2 * i * half : (2 * i + 1) * half]
        second[:, i * half : (i + 1) * half] = joint[:, (2 * i + 1) * half : (2 * i + 2) * half]
    small = [biases[...], gains[...]] + [hidden[:, i : i + LANES] for i in range(0, hidden.shape[1], LANES)]
    first[:, 3 * half :] = stack_rows(small, first.shape[0])
    rows = own_quarter(quarter.shape[0])
    quarter[:, : first.shape[1]] = first[rows, :]
    quarter[:, first.shape[1] :] = second[rows, :]


def local_call(kernel, name, shapes, arrays):
    return pl.pallas_call(
        kernel,
        out_shape=[jax.ShapeDtypeStruct(s, bf16) for s in shapes],
        compiler_params=params(),
        name=name,
    )(*arrays)


def cut(joint, biases, gains, hidden, dp):
    rows, width = joint.shape
    shapes = [(rows, width // 2 + LANES), (rows, width // 2), (rows // dp, width + LANES)]
    return local_call(cut_kernel, "cut", shapes, [joint, biases, gains, hidden])


def pack_kernel(chunks, shards, up, down, wo, q_down, q_up, v_down, v_up, *refs):
    outs, parts = refs[:chunks], refs[chunks : chunks + 2]
    down_map, up_map = refs[chunks + 2 :]
    hidden, width = down.shape
    part = hidden // chunks
    for j, out in enumerate(outs):
        for s in range(shards):
            start = s * hidden + j * part
            out[:, s * part : (s + 1) * part] = up[:, start : start + part]
        out[:, width : 2 * width] = down[j * part : (j + 1) * part, :]
    outs[0][:, 2 * width :] = wo[...]
    for out, part_ref in zip((outs[1], outs[3]), parts):
        part_ref[...] = out[own_quarter(part_ref.shape[0]), :]
    rank = q_up.shape[0]
    down_map[...] = jnp.zeros_like(down_map)
    down_map[:, :rank] = q_down[...]
    down_map[:, rank : 2 * rank] = v_down[...]
    zero = jnp.zeros(q_up.shape, f32)
    rows = [jnp.concatenate([q_up[...].astype(f32) * 8.0, zero], axis=1)]
    rows += [jnp.concatenate([zero, v_up[...].astype(f32) * 8.0], axis=1)]
    up_map[...] = stack_rows(rows, up_map.shape[0])


def pack(up, down, wo, adapters, chunks, shards, dp):
    rows, width = up.shape[0], down.shape[1]
    columns = [3 * width, 2 * width, 2 * width, 2 * width]
    shapes = [(rows, c) for c in columns] + [(rows // dp, columns[j]) for j in (1, 3)]
    shapes += [(width, LANES), (LANES, 2 * width)]
    return local_call(functools.partial(pack_kernel, chunks, shards), "pack", shapes, [up, down, wo, *adapters])


def project_slot(first, carried, shards, w, wait, ins, outs):
    rows_in, down, up = ins[:3]
    q_ref, k_ref, v_ref = outs[:3]
    half = q_ref.shape[1]
    width = 2 * half
    cols = slice(0, half) if first else slice(half, width)
    wait(0)
    if first:
        low_ref, normed_ref, vec = outs[3:6]

        @pl.when(pl.program_id(0) == 0)
        def _():
            if carried:
                rows = w.shape[0] // shards
                parts = [w[s * rows : s * rows + vec.shape[0], 3 * half :] for s in range(shards)]
                vec[...] = jnp.concatenate(parts, axis=1).astype(f32)
            else:
                vec[...] = ins[3][...]
    else:
        low_in, vec = ins[3:]
    sub = 256
    state = {}

    def norm(r):
        rr = slice(r, r + sub)
        if first:
            n, _ = normalise(rows_in[rr, :].astype(f32))
            normed = (n * vec[6:7, :] + vec[0:1, :]).astype(bf16)
            normed_ref[rr, :] = normed
        else:
            normed = rows_in[rr, :]
        state[r] = normed

    def mix(r):
        rr = slice(r, r + sub)
        normed = state.pop(r)
        k_ref[rr, :] = dot(normed, w[:, half : 2 * half]).astype(bf16)
        if first:
            low = dot(normed, down[...]).astype(bf16)
            low_ref[rr, :] = low
        else:
            low = low_in[rr, :]
        q = dot(normed, w[:, :half]) + dot(low, up[:, cols]) + vec[2:3, cols]
        q_ref[rr, :] = (q * SCORE_SCALE).astype(bf16)
        v = dot(normed, w[:, 2 * half : 3 * half]) + dot(low, up[:, width:][:, cols]) + vec[3:4, cols]
        v_ref[rr, :] = v.astype(bf16)

    pipelined(list(range(0, rows_in.shape[0], sub)), (norm, mix), (0, 1))


def heads_kernel(first, carried, shards, pairs, wholes, wait, ins, outs, scratch):
    lengths, ins = ins[0], ins[1:]
    q_ref, k_ref, v_ref = outs[:3]
    o_ref, p_ref, linv_ref = outs[-3:]
    (mask,) = scratch
    blocks = q_ref.shape[0] // LANES

    @pl.when(pl.program_id(1) == 0)
    def _():
        project_slot(first, carried, shards, wholes[0], wait, ins, outs)
        fill_masks(lengths, pl.program_id(0), mask, blocks)

    @pl.when(pl.program_id(1) != 0)
    def _():
        at = pl.multiple_of((pl.program_id(1) - 1) * pairs * PAIR, pairs * PAIR)
        attend_pairs(pairs, blocks, at, q_ref, k_ref, v_ref, o_ref, p_ref, linv_ref, mask)


def heads(weight, place, fsdp, lengths, x, down, up, vec=None, low=None, old=()):
    tokens, width = x.shape
    slots = lengths.shape[0]
    seq = tokens // slots
    blocks, heads2, pairs = seq // LANES, width // PAIR, 2
    steps = heads2 // pairs // 2
    first = low is None
    here = 0 if first else 1
    row = pl.BlockSpec((seq, width), lambda s, j, _: (s, 0))
    thin = pl.BlockSpec((seq, LANES), lambda s, j, _: (s, 0))
    half = pl.BlockSpec((seq, width // 2), lambda s, j, _: (s, here))
    group = lambda j: here * steps + jnp.maximum(j - 1, 0)
    tile = pl.BlockSpec((seq, pairs * PAIR), lambda s, j, _: (s, group(j)))
    probs = (pairs, blocks, BAND * LANES, 2 * LANES)
    sums = (pairs, blocks, 2 * LANES)
    ins = [lengths, x, down, up]
    in_specs = [pl.BlockSpec(memory_space=pltpu.SMEM), row, resident(down), resident(up)]
    outs, out_specs = [jax.ShapeDtypeStruct((tokens, width), bf16)] * 3, [half] * 3
    if first:
        outs = outs + [jax.ShapeDtypeStruct((tokens, n), bf16) for n in (LANES, width)]
        outs = outs + [jax.ShapeDtypeStruct((16, width), f32)]
        out_specs = out_specs + [thin, row, pl.BlockSpec((16, width), lambda s, j, _: (0, 0))]
    else:
        ins, in_specs = ins + [low], in_specs + [thin]
    if vec is not None:
        ins, in_specs = ins + [vec], in_specs + [resident(vec)]
    outs = outs + [
        jax.ShapeDtypeStruct((tokens, width), bf16),
        jax.ShapeDtypeStruct((slots, heads2) + probs[1:], bf16),
        jax.ShapeDtypeStruct((slots, heads2) + sums[1:], f32),
    ]
    out_specs = out_specs + [
        tile,
        pl.BlockSpec((1,) + probs, lambda s, j, _: (s, group(j), 0, 0, 0)),
        pl.BlockSpec((1,) + sums, lambda s, j, _: (s, group(j), 0, 0)),
    ]
    carried = first and vec is None
    columns = 3 * width // 2 + (LANES if carried else 0)
    return weight_call(
        functools.partial(heads_kernel, first, carried, fsdp, pairs),
        "heads",
        [(weight, (width, columns))],
        [(0, 0, columns)],
        (slots, 1 + steps),
        ins,
        in_specs,
        out_specs,
        outs,
        [pltpu.VMEM((blocks, BAND * LANES, LANES), f32)],
        place,
        9 * tokens * width * width,
        fsdp,
        old,
    )


def fill_masks(lengths, slot, mask, blocks):
    starts = []
    total = jnp.int32(0)
    for d in range(lengths.shape[1]):
        starts.append(total)
        total = total + lengths[slot, d]
    for qb in range(blocks):
        first = max(0, qb - BAND + 1)
        rows = (qb - first + 1) * LANES
        query = qb * LANES + lax.broadcasted_iota(jnp.int32, (8, LANES), 1)
        begin = jnp.zeros((8, LANES), jnp.int32)
        for start in starts:
            begin = jnp.where(query >= start, start, begin)
        key = first * LANES + lax.broadcasted_iota(jnp.int32, (rows, LANES), 0)
        ok = (key >= begin[0:1]) & (key <= query[0:1])
        mask[qb, :rows, :] = jnp.where(ok, 0.0, MASKED)


def half_lanes():
    return lax.broadcasted_iota(jnp.int32, (LANES, LANES), 1) < 64


def half_rows():
    return lax.broadcasted_iota(jnp.int32, (LANES, LANES), 0) < 64


def split_heads(x, left):
    zero = jnp.zeros_like(x)
    return jnp.concatenate([jnp.where(left, x, zero), jnp.where(left, zero, x)], axis=0)


def pipelined(units, stages, lags):
    for t in range(len(units) + lags[-1]):
        for stage, lag in zip(stages, lags):
            if 0 <= t - lag < len(units):
                stage(units[t - lag])


def geometry(qb):
    first = max(0, qb - BAND + 1)
    return first * LANES, (qb - first + 1) * LANES


def attend_pairs(pairs, blocks, at, q_ref, k_ref, v_ref, o_ref, p_ref, linv_ref, mask):
    left, top = half_lanes(), half_rows()
    scores, probs = {}, {}

    def score(unit):
        pair, qb = unit
        cols = pl.ds(at + pair * PAIR, PAIR)
        key0, rows = geometry(qb)
        q = split_heads(q_ref[qb * LANES : (qb + 1) * LANES, cols], left)
        scores[unit] = dot_nt(k_ref[key0 : key0 + rows, cols], q)

    def soften(unit):
        pair, qb = unit
        key0, rows = geometry(qb)
        bias = mask[qb, :rows, :]
        s = scores.pop(unit) + jnp.concatenate([bias, bias], axis=1)
        p = jnp.exp2(s - jnp.max(s, axis=0, keepdims=True))
        linv = 1.0 / jnp.sum(p, axis=0, keepdims=True)
        linv_ref[0, pair, qb : qb + 1, :] = linv
        low = p.astype(bf16)
        p_ref[0, pair, qb, :rows, :] = low
        probs[unit] = (low, linv)

    def mix(unit):
        pair, qb = unit
        key0, rows = geometry(qb)
        low, linv = probs.pop(unit)
        o = dot_tn(v_ref[key0 : key0 + rows, pl.ds(at + pair * PAIR, PAIR)], low)
        o = jnp.where(top, o[:, :LANES] * linv[:, :LANES], o[:, LANES:] * linv[:, LANES:])
        o_ref[qb * LANES : (qb + 1) * LANES, pair * PAIR : (pair + 1) * PAIR] = o.T.astype(bf16)

    units = [(pair, qb) for qb in range(blocks) for pair in range(pairs)]
    pipelined(units, (score, soften, mix), (0, 2, 5))


def attend_back_kernel(
    pairs, blocks, q_ref, k_ref, v_ref, g_ref, o_ref, p_ref, linv_ref, low, normed, up, *refs
):
    dq_ref, dk_ref, dv_ref, glow_ref, grads, dk_sum, dv_sum, glow_sum = refs
    left, top = half_lanes(), half_rows()
    ones = jnp.ones((BAND * LANES, LANES), bf16)
    dk_sum[...] = jnp.zeros_like(dk_sum)
    dv_sum[...] = jnp.zeros_like(dv_sum)
    first, second = {}, {}

    def grad_probs(unit):
        pair, qb = unit
        cols = slice(pair * PAIR, (pair + 1) * PAIR)
        key0, rows = geometry(qb)
        here = slice(qb * LANES, (qb + 1) * LANES)
        linv = linv_ref[0, pair, qb : qb + 1, :]
        linv = jnp.where(top, linv[:, :LANES], linv[:, LANES:]).T
        g = g_ref[here, cols].astype(f32) * linv
        delta = split_heads(-(g * o_ref[here, cols].astype(f32)).astype(bf16), left)
        g = split_heads(g.astype(bf16), left)
        values = jnp.concatenate([v_ref[key0 : key0 + rows, cols], ones[:rows]], axis=1)
        first[unit] = (dot_nt(values, jnp.concatenate([g, delta], axis=1)), g)

    def grad_values(unit):
        pair, qb = unit
        cols = slice(pair * PAIR, (pair + 1) * PAIR)
        key0, rows = geometry(qb)
        dp, g = first.pop(unit)
        low = p_ref[0, pair, qb, :rows, :]
        second[unit] = low * dp.astype(bf16)
        dv_sum[key0 : key0 + rows, cols] += dot(low, g)

    def grad_queries_keys(unit):
        pair, qb = unit
        cols = slice(pair * PAIR, (pair + 1) * PAIR)
        key0, rows = geometry(qb)
        here = slice(qb * LANES, (qb + 1) * LANES)
        ds = second.pop(unit)
        dk_sum[key0 : key0 + rows, cols] += dot(ds, split_heads(q_ref[here, cols], left))
        dq = dot_tn(k_ref[key0 : key0 + rows, cols], ds)
        dq = jnp.where(top, dq[:, :LANES], dq[:, LANES:]) * 0.125
        dq_ref[here, cols] = dq.T.astype(bf16)

    units = [(pair, qb) for qb in range(blocks) for pair in range(pairs)]
    pipelined(units, (grad_probs, grad_values, grad_queries_keys), (0, 2, 4))
    dk_ref[...] = (dk_sum[...] * (0.125 / SCORE_SCALE)).astype(bf16)
    dv_ref[...] = dv_sum[...].astype(bf16)

    slot, step, last = pl.program_id(0), pl.program_id(1), pl.num_programs(1) - 1
    width = normed.shape[1]
    at = pl.multiple_of(step * pairs * PAIR, pairs * PAIR)
    here = pl.ds(at, pairs * PAIR)
    part = [dot_tn(low[...], dq_ref[...])[0:4], dot_tn(low[...], dv_ref[...])[4:8]]
    part = jnp.concatenate(part, axis=0) * 8.0
    grads[0:8, here] = jnp.where(slot == 0, part, grads[0:8, here] + part)
    glow = dot_nt(dq_ref[...], up[:, here]) + dot_nt(dv_ref[...], up[:, pl.ds(width + at, pairs * PAIR)])
    glow_sum[...] = jnp.where(step == 0, glow, glow_sum[...] + glow)

    @pl.when(step == last)
    def _():
        glow = glow_sum[...].astype(bf16)
        glow_ref[...] = glow
        part = dot_tn(glow, normed[...])[0:8]
        grads[8:16, :] = jnp.where(slot == 0, part, grads[8:16, :] + part)


def attend_back(slots, q, k, v, g, o, p, linv, low, normed, up):
    tokens, width = q.shape
    seq = tokens // slots
    blocks, heads2, pairs = seq // LANES, width // PAIR, 2
    rows = BAND * LANES
    tile = pl.BlockSpec((seq, pairs * PAIR), lambda s, h: (s, h))
    thin = pl.BlockSpec((seq, LANES), lambda s, h: (s, 0))
    return pl.pallas_call(
        functools.partial(attend_back_kernel, pairs, blocks),
        grid=(slots, heads2 // pairs),
        in_specs=[tile] * 5
        + [
            pl.BlockSpec((1, pairs, blocks, rows, 2 * LANES), lambda s, h: (s, h, 0, 0, 0)),
            pl.BlockSpec((1, pairs, blocks, 2 * LANES), lambda s, h: (s, h, 0, 0)),
            thin,
            pl.BlockSpec((seq, width), lambda s, h: (s, 0)),
            resident(up),
        ],
        out_specs=[tile] * 3 + [thin, pl.BlockSpec((16, width), lambda s, h: (0, 0))],
        scratch_shapes=[pltpu.VMEM((seq, pairs * PAIR), f32)] * 2 + [pltpu.VMEM((seq, LANES), f32)],
        out_shape=[jax.ShapeDtypeStruct(q.shape, bf16)] * 3
        + [jax.ShapeDtypeStruct((tokens, LANES), bf16), jax.ShapeDtypeStruct((16, width), f32)],
        compiler_params=params(),
        cost_estimate=pl.CostEstimate(flops=14 * tokens * width * width // COST, bytes_accessed=2**20, transcendentals=0),
        name="attend_back",
    )(q, k, v, g, o, p, linv, low, normed, up)


def feed_chunk(wait, first, normed, cot, w, bias):
    width = cot.shape[1]
    wait(first)
    wait(first + 1)
    size = width // 4
    acts, grads = [], []
    for i in range(0, width, size):
        grad = dot_nt(cot, w[i : i + size, width : 2 * width])
        act, slope = gelu_and_slope(dot(normed, w[:, i : i + size]) + bias[:, i : i + size])
        acts.append(act.astype(bf16))
        grads.append((slope * grad).astype(bf16))
    o = dot(jnp.concatenate(acts, axis=1), w[:, width : 2 * width])
    return o, dot_nt(jnp.concatenate(grads, axis=1), w[:, :width])


def feed_first_kernel(wholes, wait, ins, outs, _):
    tok, att, cot, vec = ins
    h1_ref, normed_ref, o_ref, g_ref = outs
    width = tok.shape[1]
    wait(0)
    h1 = tok[...].astype(f32) + dot(att[...], wholes[0][:, 2 * width :]) + vec[4:5, :]
    h1_ref[...] = h1
    n, _ = normalise(h1)
    normed = (n * vec[7:8, :] + vec[1:2, :]).astype(bf16)
    normed_ref[...] = normed
    o_ref[...], g_ref[...] = feed_chunk(wait, 1, normed, cot[...], wholes[0], vec[8:9, :])
    o, g = feed_chunk(wait, 3, normed, cot[...], wholes[1], vec[9:10, :])
    o_ref[...] += o
    g_ref[...] += g


def feed_last_kernel(wholes, wait, ins, outs, scratch):
    h1, normed, old_o, old_g, cot, vec = ins
    out_ref, gh_ref, ga_ref = outs
    o_sum, g_sum = scratch
    width = cot.shape[1]
    o, g = feed_chunk(wait, 0, normed[...], cot[...], wholes[0], vec[10:11, :])
    o_sum[...] = old_o[...] + o
    g_sum[...] = old_g[...] + g
    o, g = feed_chunk(wait, 2, normed[...], cot[...], wholes[1], vec[11:12, :])
    x = h1[...]
    out_ref[...] = (x + (o_sum[...] + o) + vec[5:6, :]).astype(bf16)
    n, r = normalise(x)
    grad = cot[...].astype(f32) + norm_back(n, r, (g_sum[...] + g) * vec[7:8, :])
    low = grad.astype(bf16)
    gh_ref[...] = low
    wait(4)
    ga_ref[...] = dot_nt(low, wholes[2][:, 2 * width :]).astype(bf16)


def feed_call(kernel, name, weights, order, place, fsdp, rowwise, vec, out_types, sums):
    tokens, width = rowwise[0].shape
    rows = 512
    row = pl.BlockSpec((rows, width), lambda i, _: (i, 0))
    return weight_call(
        kernel,
        name,
        weights,
        order,
        (tokens // rows,),
        rowwise + [vec],
        [row] * len(rowwise) + [resident(vec)],
        [row] * len(out_types),
        [jax.ShapeDtypeStruct((tokens, width), t) for t in out_types],
        [pltpu.VMEM((rows, width), f32)] * sums,
        place,
        18 * tokens * width * width,
        fsdp,
    )


def feed_first(feeds, place, fsdp, tok, att, cot, vec):
    width = tok.shape[1]
    weights = [(feeds[0], (width, 3 * width)), (feeds[1], (width, 2 * width))]
    order = [(0, 2 * width, width), (0, width, width), (0, 0, width), (1, width, width), (1, 0, width)]
    types = [f32, bf16, f32, f32]
    return feed_call(feed_first_kernel, "feed_first", weights, order, place, fsdp, [tok, att, cot], vec, types, 0)


def feed_last(feeds, place, fsdp, h1, normed, o, g, cot, vec):
    width = cot.shape[1]
    weights = [(feeds[2], (width, 2 * width)), (feeds[3], (width, 2 * width)), (feeds[0], (width, 3 * width))]
    order = [(0, width, width), (0, 0, width), (1, width, width), (1, 0, width), (2, 2 * width, width)]
    rowwise = [h1, normed, o, g, cot]
    return feed_call(feed_last_kernel, "feed_last", weights, order, place, fsdp, rowwise, vec, [bf16] * 3, 2)


def input_kernel(wholes, wait, ins, outs, _):
    tok, gh, dq, dk, dv, glow, down, vec = ins
    (out_ref,) = outs
    half = tok.shape[1] // 2
    g = dot_nt(glow[...], down[...])
    for i, w in enumerate(wholes):
        wait(i)
        cols = slice(i * half, (i + 1) * half)
        g = g + dot_nt(dq[:, cols], w[:, :half])
        g = g + dot_nt(dk[:, cols], w[:, half : 2 * half])
        g = g + dot_nt(dv[:, cols], w[:, 2 * half : 3 * half])
    n, r = normalise(tok[...].astype(f32))
    out_ref[...] = (gh[...].astype(f32) + norm_back(n, r, g * vec[6:7, :])).astype(bf16)


def input_grad(joint, place, fsdp, tok, gh, dq, dk, dv, glow, down, vec):
    tokens, width = tok.shape
    rows = 512
    row = pl.BlockSpec((rows, width), lambda i, _: (i, 0))
    thin = pl.BlockSpec((rows, LANES), lambda i, _: (i, 0))
    return weight_call(
        input_kernel,
        "input_grad",
        [(w, (width, 3 * width // 2)) for w in joint],
        [(0, 0, 3 * width // 2), (1, 0, 3 * width // 2)],
        (tokens // rows,),
        [tok, gh, dq, dk, dv, glow, down, vec],
        [row] * 5 + [thin, resident(down), resident(vec)],
        [row],
        [jax.ShapeDtypeStruct((tokens, width), bf16)],
        [],
        place,
        6 * tokens * width * width,
        fsdp,
    )[0]


def per_device(
    tokens,
    document_length_list,
    joint_projection_weight,
    attention_out_weight,
    feed_up_weight,
    feed_down_weight,
    frozen_norm_gains,
    biases,
    hidden_up_bias,
    query_down_adapter,
    query_up_adapter,
    value_down_adapter,
    value_up_adapter,
    cotangent,
):
    micro, local, seq, width = tokens.shape
    slots = micro * local
    shards = width // joint_projection_weight.shape[0]
    hidden = feed_down_weight.shape[0]
    tok = tokens.reshape(slots * seq, width)
    cot = cotangent.reshape(slots * seq, width)
    lengths = document_length_list.reshape(slots, -1)

    dp = lax.axis_size("dp")
    place = jnp.stack([lax.axis_index("dp"), lax.axis_index("fsdp")]).astype(jnp.int32)
    chunks = 4
    part = hidden // chunks
    stepped = dp == 4 and shards == 8 and part == LANES and width == shards * LANES

    def gather(x):
        return lax.all_gather(x, "fsdp", axis=0, tiled=True)

    adapters = [query_down_adapter, query_up_adapter, value_down_adapter, value_up_adapter]
    if stepped:
        hidden_bias = hidden_up_bias.reshape(1, -1)
        a, b, quarter = cut(joint_projection_weight, biases, frozen_norm_gains, hidden_bias, dp)
        link = Gather(dp, shards)
        near = link.step_1(quarter)
        up, down = after_all([feed_up_weight, feed_down_weight], quarter)
        *packed, down_map, up_map = pack(up, down, attention_out_weight, adapters, chunks, shards, dp)
        c0, c1, c2, c3, c1_part, c3_part = packed
        split = a.shape[1]
        a_far = link.step_2(jnp.concatenate([x[:, :split] for x in near], axis=0))
        c0, c1_part = after_all([c0, c1_part], near)
        feeds = [[gather(c0)]]
        c1_near = link.step_1(c1_part)
        near = jnp.concatenate([x[:, split:] for x in near], axis=0)
        b_far = link.step_2(after(near, a_far))
        joint = [[a, link.swap(a)] + link.step_3(a_far) + [0]]
        vec = None
    else:
        small = jnp.concatenate([biases, frozen_norm_gains], axis=0)
        small = lax.all_gather(small, "fsdp", axis=1, tiled=True)
        hidden_bias = lax.all_gather(hidden_up_bias, "fsdp", axis=0, tiled=False)
        hidden_bias = [hidden_bias[:, j * part : (j + 1) * part].reshape(1, -1) for j in range(chunks)]
        vec = jnp.concatenate([small] + hidden_bias, axis=0)
        vec = jnp.pad(vec, ((0, 16 - 8 - chunks), (0, 0))).astype(f32)
        third = [width * i // 2 for i in range(6)]
        joint = []
        for i in (0, 1):
            cols = [lax.slice_in_dim(joint_projection_weight, t, t + width // 2, axis=1) for t in third[i::2]]
            joint.append([gather(jnp.concatenate(cols, axis=1))])
        up_parts = feed_up_weight.reshape(-1, shards, chunks, part)
        feeds = []
        for j in range(chunks):
            cols = [up_parts[:, :, j, :].reshape(-1, shards * part), feed_down_weight[j * part : (j + 1) * part]]
            if j == 0:
                cols.append(attention_out_weight)
            feeds.append([gather(jnp.concatenate(cols, axis=1))])
        rank = query_down_adapter.shape[1]
        down_map = jnp.concatenate([query_down_adapter, value_down_adapter], axis=1)
        down_map = jnp.pad(down_map, ((0, 0), (0, LANES - 2 * rank)))
        zero = jnp.zeros_like(query_up_adapter)
        up_map = jnp.concatenate(
            [
                jnp.concatenate([query_up_adapter, zero], axis=1),
                jnp.concatenate([zero, value_up_adapter], axis=1),
            ],
            axis=0,
        )
        up_map = jnp.pad(up_map * 8, ((0, LANES - 2 * rank), (0, 0))).astype(bf16)

    q, k, v, low, normed, vec, *kept = heads(joint[0], place, shards, lengths, tok, down_map, up_map, vec)
    if stepped:
        b_far, *c1_near, q, c3_part = after_all([b_far] + c1_near + [q, c3_part], low)
        joint.append([b, link.swap(b)] + link.step_3(b_far) + [0])
        c1_far = link.step_2(jnp.concatenate(c1_near, axis=0))
        c3_near = link.step_1(c3_part)
    old = [q, k, v] + kept
    q, k, v, att, probs, linv = heads(joint[1], place, shards, lengths, normed, down_map, up_map, vec, low, old)
    if stepped:
        c1_far, *c3_near, att, c2 = after_all([c1_far] + c3_near + [att, c2], linv)
        c3_far = link.step_2(jnp.concatenate(c3_near, axis=0))
        feeds += [[c1, link.swap(c1)] + link.step_3(c1_far) + [0], [gather(c2)]]
    h1, normed_2, o, g = feed_first(feeds, place, shards, tok, att, cot, vec)
    if stepped:
        c3_far, o = after_all([c3_far, o], h1)
        feeds.append([c3, link.swap(c3)] + link.step_3(c3_far) + [0])
    out, gh, ga = feed_last(feeds, place, shards, h1, normed_2, o, g, cot, vec)

    dq, dk, dv, glow, grads = attend_back(slots, q, k, v, ga, att, probs, linv, low, normed, up_map)
    if stepped:
        total = Gather(dp, shards)
        grads = grads + total.move(grads, lambda d, f: (d, f ^ 1))
        a, b, c = [total.move(grads, lambda d, f, e=e: (d ^ e, f)) for e in (1, 2, 3)]
        grads = (grads + a) + (b + c)
        a, b, c = [total.move(grads, lambda d, f, k=k: (d, (f + 2 * k) % shards)) for k in (1, 2, 3)]
        dq = after(dq, grads)
        grad_in = input_grad(joint, place, shards, tok, gh, dq, dk, dv, glow, down_map, vec)
        a, b, c = after_all([a, b, c], grad_in)
        grads = (grads + b) + (a + c)
    else:
        grads = jnp.sum(lax.all_gather(grads, ("dp", "fsdp"), axis=0, tiled=False), axis=0)
        grad_in = input_grad(joint, place, shards, tok, gh, dq, dk, dv, glow, down_map, vec)
    return (
        out.reshape(tokens.shape),
        grad_in.reshape(tokens.shape),
        grads[8:12].T,
        grads[0:4],
        grads[12:16].T,
        grads[4:8],
    )


def solution(mesh):
    slots = P(None, ("dp", "fsdp"), None, None)
    return jax.shard_map(
        per_device,
        mesh=mesh,
        in_specs=(
            slots,
            P(None, ("dp", "fsdp"), None),
            P("fsdp", None),
            P("fsdp", None),
            P("fsdp", None),
            P("fsdp", None),
            P(None, "fsdp"),
            P(None, "fsdp"),
            P("fsdp"),
            P(),
            P(),
            P(),
            P(),
            slots,
        ),
        out_specs=(slots, slots, P(), P(), P(), P()),
        check_vma=False,
    )
```

time: 491 us -> 360 us (0.73)
  waiting for transfers between devices: 211 us -> 21.5 us
  starting transfers between devices: 0.44 us -> 35.1 us
  Pallas kernels: 228 us -> 246 us
    all_gather x11 -> x2, waiting for transfers between devices: 207 us -> 0.01 us  [gather(): return lax.all_gather(x, 'fsdp', axis=0, tiled=True)]
    ppermute x0 -> x24, starting transfers between devices: none -> 23.5 us  [move(): lax.ppermute(x, ('dp', 'fsdp'), ring_pairs(self.dp, self.fsdp, where))]
    ppermute x0 -> x24, waiting for transfers between devices: none -> 21.5 us  [move(): lax.ppermute(x, ('dp', 'fsdp'), ring_pairs(self.dp, self.fsdp, where))]
    all_to_all x0 -> x1, blocking collectives: none -> 19.5 us  [step_2(): return lax.all_to_all(near, 'dp', 0, 0, tiled=False)]
    all_gather x1 -> x0, blocking collectives: 16.6 us -> none  [per_device(): small = lax.all_gather(small, 'fsdp', axis=0, tiled=False).astype(f32)]
    all_to_all x0 -> x3, starting transfers between devices: none -> 11.5 us  [step_2(): return lax.all_to_all(near, 'dp', 0, 0, tiled=False)]
    pallas_call x8 -> x7, Pallas kernels: 199 us -> 210 us  [the longest x5 205 us: weight_call(): pl.pallas_call(body, grid_spec=pltpu.PrefetchScalarGridSpec(num_scalar_pr...]
    slice x3 -> x6, local copies, waits for them, and re-layouts: 7.51 us -> 0.05 us  [the longest x3 0.03 us: per_device(): a_far = link.step_2(jnp.concatenate([x[:, :split] for x in near], axis=0))]
  transfers between devices with their start and end apart: 11 -> 29, of which waited for: 9 -> 7; matrix products, arithmetic and copies ran while one was open for 3% -> 3% of each run, Pallas kernels for 32% -> 39%
where the time goes in v2:
time: 360 us; the launch traced here: 356 us
  Pallas kernels  246 us (68%)
  starting transfers between devices  35.1 us (10%)
  waiting for transfers between devices  21.5 us (6%)
  blocking collectives  19.5 us (5%)
  between operations  14.6 us (4%)
  local copies, waits for them, and re-layouts  14.3 us (4%)
  other arithmetic  4.47 us (1%)
    pallas_call x5, Pallas kernels, weight_call(): pl.pallas_call(body, grid_spec=pltpu.PrefetchScalarGridSpec(num_scalar_pr...  205 us
    pallas_call x1, Pallas kernels, attend_back(): pl.pallas_call(functools.partial(attend_back_kernel, pairs, blocks), grid...  35.9 us
    ppermute x24, starting transfers between devices, move(): lax.ppermute(x, ('dp', 'fsdp'), ring_pairs(self.dp, self.fsdp, where))  23.5 us
    ppermute x24, waiting for transfers between devices, move(): lax.ppermute(x, ('dp', 'fsdp'), ring_pairs(self.dp, self.fsdp, where))  21.5 us
    all_to_all x1, blocking collectives, step_2(): return lax.all_to_all(near, 'dp', 0, 0, tiled=False)  19.5 us
    all_to_all x3, starting transfers between devices, step_2(): return lax.all_to_all(near, 'dp', 0, 0, tiled=False)  11.5 us
    unnamed x28, local copies, waits for them, and re-layouts  8.39 us
  transfers between devices with their start and end apart: 29, of which 7 were waited for; matrix products, arithmetic and copies ran while one was open for 3% of the time, Pallas kernels for 39%

profile of v2, /device:TPU:0, one launch (start us, length us, event | category | flops | bytes accessed | tf_op | source)
XLA Modules:
  0.0 355.8 jit_solution(10273278566517578993)
XLA Ops:
  7.2 1.3 reshape.34.hidden
  8.5 2.2 cut.1
  10.6 5.0 %collective-permute-start.2 = (bf16[32,3200]{1,0:T(8,128)(2,1)}, bf16[32,3200]{1,0:T(8,128)(2,1)S(1)}, u32[]{:S(2)}, u32[]{:S(2)}) collective-permute-start(bf16[32,3200]{1,0:T(8,128)(2,1)} %get-tuple-element.67), channel_id=1, source_target_pairs={{0,6},{1,7},{2,0},{3,1},{4,2},{5,3},{6,4},{7,5},{8,14},{9,15},{10,... | collective-permute-start | bytes 614408 | tf_op jit(solution)/shard_map/ppermute | solution.py:87
  15.7 1.0 collective-permute-start
  16.7 1.6 copy.26.q_down
  18.3 1.6 copy.27.v_down
  19.8 3.6 %pack.1 = (bf16[128,3072]{1,0:T(8,128)(2,1)}, bf16[128,2048]{1,0:T(8,128)(2,1)}, bf16[128,2048]{1,0:T(8,128)(2,1)}, bf16[128,2048]{1,0:T(8,128)(2,1)}, bf16[32,2...) custom-call(bf16[128,4096]{1,0:T(8,128)(2,1)} %up, ...), custom_call_target="tpu_custom_call" | custom-call | tf_op jit(solution)/shard_map/pack/pallas_call | solution.py:215
  23.5 9.8 %collective-permute-done.1 = bf16[32,3200]{1,0:T(8,128)(2,1)S(1)} collective-permute-done((bf16[32,3200]{1,0:T(8,128)(2,1)}, bf16[32,3200]{1,0:T(8,128)(2,1)S(1)}, u32[]{:S(2)}, u32[]{:S(2)}) %collective-permute-start.1) | collective-permute-done | bytes 204832 | tf_op jit(solution)/shard_map/ppermute | solution.py:87
  33.5 19.5 %all_to_all.20.refs_2_ = bf16[4,96,1664]{2,1,0:T(8,128)(2,1)S(1)} all-to-all(bf16[4,96,1664]{2,1,0:T(8,128)(2,1)S(1)} %broadcast_in_dim.8), channel_id=1, replica_groups=mesh['dp'=4,'fsdp'=8] {'dp'}, dimensions={0} | all-to-all | bytes 2555904 | tf_op jit(solution)/shard_map/all_to_all | solution.py:95
  53.0 1.2 broadcast_in_dim.9
  54.3 3.5 all-to-all-start.1
  57.8 0.5 collective-permute-start.6
  58.3 0.6 pad_add_fusion.place_ref
  58.8 3.1 collective-permute-start.4
  61.9 2.0 collective-permute-start.3
  64.0 0.8 copy-done.8
  64.7 29.4 %heads.2 = (bf16[2048,1024]{1,0:T(8,128)(2,1)}, bf16[2048,1024]{1,0:T(8,128)(2,1)}, bf16[2048,1024]{1,0:T(8,128)(2,1)}, bf16[2048,128]{1,0:T(8,128)(2,1)}, bf16[...) custom-call(s32[2]{0:T(128)} %pad_add_fusion.place_ref, ...), custom_call_target="tpu_custom_call" | custom-call | flops 2415919104 | bytes 1048576 | tf_op jit(solution)/shard_map/heads/pallas_call | solution.py:171
  94.2 0.6 copy-done.11
  94.8 0.6 copy-done.12
  95.6 1.4 pad_maximum_fusion
  97.0 1.3 broadcast_in_dim.10
  98.3 3.8 %all-to-all-start.2 = ((bf16[4,96,2048]{2,1,0:T(8,128)(2,1)}), bf16[4,96,2048]{2,1,0:T(8,128)(2,1)S(1)}, u32[]{:S(2)}, u32[]{:S(2)}) async-start(bf16[4,96,2048]{2,1,0:T(8,128)(2,1)} %broadcast_in_dim.10), calls=%async_computation.2 | async-start | bytes 3145728 | tf_op jit(solution)/shard_map/all_to_all | solution.py:95
  102.2 1.8 collective-permute-start.10
  104.0 0.9 collective-permute-start.8
  104.9 0.7 copy-done.5
  105.7 25.9 %heads.3 = (bf16[2048,1024]{1,0:T(8,128)(2,1)}, bf16[2048,1024]{1,0:T(8,128)(2,1)}, bf16[2048,1024]{1,0:T(8,128)(2,1)}, bf16[2048,1024]{1,0:T(8,128)(2,1)}, bf16...) custom-call(s32[2]{0:T(128)} %pad_add_fusion.place_ref, ...), custom_call_target="tpu_custom_call", output_to_operand_aliasing={{0}: (11, {}), {1}: (12, {}), {2}: (13, {}), {3}: (14, {}),... | custom-call | flops 2415919104 | bytes 1048576 | tf_op jit(solution)/shard_map/heads/pallas_call | solution.py:171
  131.6 0.6 copy-done.9
  132.3 0.6 copy-done.10
  133.0 1.5 pad_maximum_fusion.1
  134.6 1.3 broadcast_in_dim.11
  135.9 4.2 %all-to-all-start.3 = ((bf16[4,96,2048]{2,1,0:T(8,128)(2,1)}), bf16[4,96,2048]{2,1,0:T(8,128)(2,1)S(1)}, u32[]{:S(2)}, u32[]{:S(2)}) async-start(bf16[4,96,2048]{2,1,0:T(8,128)(2,1)} %broadcast_in_dim.11), calls=%async_computation.3 | async-start | bytes 3145728 | tf_op jit(solution)/shard_map/all_to_all | solution.py:95
  140.1 2.2 collective-permute-done.14.refs_2_
  142.4 54.6 %feed_first.1 = (f32[2048,1024]{1,0:T(8,128)}, bf16[2048,1024]{1,0:T(8,128)(2,1)}, f32[2048,1024]{1,0:T(8,128)}, f32[2048,1024]{1,0:T(8,128)}) custom-call(s32[2]{0:T(128)} %pad_add_fusion.place_ref, bf16[1024,3072]{1,0:T(8,128)(2,1)} %all-gather.5.cloned.1.call-done.refs_0_.refs_5_, bf16[128,2048]{1,0:T(8,128)(2,1)} %get-tuple-element.103.refs_1_, ...), custom_call_target="tpu_custom_call" | custom-call | flops 4831838208 | bytes 1048576 | tf_op jit(solution)/shard_map/feed_first/pallas_call | solution.py:171
  197.6 4.0 %collective-permute-done.13.refs_2_ = bf16[128,2048]{1,0:T(8,128)(2,1)} collective-permute-done((bf16[128,2048]{1,0:T(8,128)(2,1)}, bf16[128,2048]{1,0:T(8,128)(2,1)}, u32[]{:S(2)}, u32[]{:S(2)}) %collective-permute-start.13) | collective-permute-done | bytes 524320 | tf_op jit(solution)/shard_map/ppermute | solution.py:87
  201.6 1.2 copy-done.6
  202.8 67.8 %feed_last.1 = (bf16[2048,1024]{1,0:T(8,128)(2,1)}, bf16[2048,1024]{1,0:T(8,128)(2,1)}, bf16[2048,1024]{1,0:T(8,128)(2,1)}) custom-call(s32[2]{0:T(128)} %pad_add_fusion.place_ref, bf16[1024,2048]{1,0:T(8,128)(2,1)} %all-gather.3.cloned.1.call-done.refs_0_, bf16[128,2048]{1,0:T(8,128)(2,1)} %get-tuple-element.98.refs_1_, ...), custom_call_target="tpu_custom_call" | custom-call | flops 4831838208 | bytes 1048576 | tf_op jit(solution)/shard_map/feed_last/pallas_call | solution.py:171
  270.6 35.9 %attend_back.1 = (bf16[2048,1024]{1,0:T(8,128)(2,1)}, bf16[2048,1024]{1,0:T(8,128)(2,1)}, bf16[2048,1024]{1,0:T(8,128)(2,1)}, bf16[2048,128]{1,0:T(8,128)(2,1)}, f32[16,1024]{1,0:T(8,128)}) custom-call(bf16[2048,1024]{1,0:T(8,128)(2,1)} %get-tuple-element.114.q_ref, bf16[2048,1024]{1,0:T(8,128)(2,1)} %get-tuple-element.115.k_ref, ...), custom_call_target="tpu_custom_call" | custom-call | flops 3758096384 | bytes 1048576 | tf_op jit(solution)/shard_map/attend_back/pallas_call | solution.py:535
  306.8 1.3 collective-permute-done.17
  308.1 0.9 add.21
  308.9 2.9 collective-permute-start.20
  311.8 0.5 collective-permute-start.19
  312.5 1.9 collective-permute-done.20
  314.3 1.8 collective-permute-done.19
  316.1 0.5 collective-permute-done.18
  316.6 3.1 collective-permute-start.23
  319.7 1.2 collective-permute-start.22
  321.2 26.9 %input_grad.1 = bf16[2048,1024]{1,0:T(8,128)(2,1)} custom-call(s32[2]{0:T(128)} %pad_add_fusion.place_ref, bf16[128,1664]{1,0:T(8,128)(2,1)} %get-tuple-element.74.refs_0_, bf16[128,1664]{1,0:T(8,128)(2,1)} %copy-done.8, bf16[4,96,1664]{2,1,0:T(8,128)(2,1)} %copy-done.3, bf16[4,96,1664]{2,1,0:T(8,128)(2,1)} %collective-permute-done.7.refs_3_, ...), custom_call_target="tpu_custom_call" | custom-call | flops 1610612736 | bytes 1048576 | tf_op jit(solution)/shard_map/input_grad/pallas_call | solution.py:171
  348.1 0.6 fusion
  (69 shorter events, 1.9 us)
Async XLA Ops:
  7.2 135.2 %all-gather.5.cloned.1.call-start = ((), (), s32[]{:S(2)}) async-start(), calls=%async_computation.5 | async-start | bytes 7077888 | tf_op jit(solution)/shard_map/all_gather | solution.py:711
  10.6 12.9 %collective-permute-start.2 = (bf16[32,3200]{1,0:T(8,128)(2,1)}, bf16[32,3200]{1,0:T(8,128)(2,1)S(1)}, u32[]{:S(2)}, u32[]{:S(2)}) collective-permute-start(bf16[32,3200]{1,0:T(8,128)(2,1)} %get-tuple-element.67), channel_id=1, source_target_pairs={{0,6},{1,7},{2,0},{3,1},{4,2},{5,3},{6,4},{7,5},{8,14},{9,15},{10,... | collective-permute-start | bytes 614408 | tf_op jit(solution)/shard_map/ppermute | solution.py:87
  15.7 17.6 %collective-permute-start.1 = (bf16[32,3200]{1,0:T(8,128)(2,1)}, bf16[32,3200]{1,0:T(8,128)(2,1)S(1)}, u32[]{:S(2)}, u32[]{:S(2)}) collective-permute-start(bf16[32,3200]{1,0:T(8,128)(2,1)} %get-tuple-element.67), channel_id=1, source_target_pairs={{0,4},{1,5},{2,6},{3,7},{4,0},{5,1},{6,2},{7,3},{8,12},{9,13},{10,... | collective-permute-start | bytes 614408 | tf_op jit(solution)/shard_map/ppermute | solution.py:87
  15.7 17.6 %collective-permute-start = (bf16[32,3200]{1,0:T(8,128)(2,1)}, bf16[32,3200]{1,0:T(8,128)(2,1)S(1)}, u32[]{:S(2)}, u32[]{:S(2)}) collective-permute-start(bf16[32,3200]{1,0:T(8,128)(2,1)} %get-tuple-element.67), channel_id=1, source_target_pairs={{0,2},{1,3},{2,4},{3,5},{4,6},{5,7},{6,0},{7,1},{8,10},{9,11},{10,... | collective-permute-start | bytes 614408 | tf_op jit(solution)/shard_map/ppermute | solution.py:87
  33.4 24.4 %copy-start.7 = (bf16[128,1664]{1,0:T(8,128)(2,1)S(1)}, bf16[128,1664]{1,0:T(8,128)(2,1)}, u32[]{:S(2)}) copy-start(bf16[128,1664]{1,0:T(8,128)(2,1)} %get-tuple-element.74.refs_0_) | copy-start | bytes 1277956
  53.0 11.0 %copy-start.3 = (bf16[4,96,1664]{2,1,0:T(8,128)(2,1)}, bf16[4,96,1664]{2,1,0:T(8,128)(2,1)S(1)}, u32[]{:S(2)}) copy-start(bf16[4,96,1664]{2,1,0:T(8,128)(2,1)S(1)} %all_to_all.20.refs_2_) | copy-start | bytes 3833860
  53.0 11.0 %collective-permute-start.7 = (bf16[4,96,1664]{2,1,0:T(8,128)(2,1)S(1)}, bf16[4,96,1664]{2,1,0:T(8,128)(2,1)}, u32[]{:S(2)}, u32[]{:S(2)}) collective-permute-start(bf16[4,96,1664]{2,1,0:T(8,128)(2,1)S(1)} %all_to_all.20.refs_2_), channel_id=1, source_target_pairs={{0,1},{1,0},{2,3},{3,2},{4,5},{5,4},{6,7},{7,6},{8,9},{9,8},{10,11... | collective-permute-start | bytes 3833864 | tf_op jit(solution)/shard_map/ppermute | solution.py:87
  54.3 41.2 %all-to-all-start.1 = ((bf16[4,96,1536]{2,1,0:T(8,128)(2,1)}), bf16[4,96,1536]{2,1,0:T(8,128)(2,1)S(1)}, u32[]{:S(2)}, u32[]{:S(2)}) async-start(bf16[4,96,1536]{2,1,0:T(8,128)(2,1)} %broadcast_in_dim.9), calls=%async_computation.1 | async-start | bytes 2359296 | tf_op jit(solution)/shard_map/all_to_all | solution.py:95
  57.8 6.1 %collective-permute-start.6 = (bf16[128,1664]{1,0:T(8,128)(2,1)S(1)}, bf16[128,1664]{1,0:T(8,128)(2,1)S(1)}, u32[]{:S(2)}, u32[]{:S(2)}) collective-permute-start(bf16[128,1664]{1,0:T(8,128)(2,1)S(1)} %copy-done.7), channel_id=1, source_target_pairs={{0,1},{1,0},{2,3},{3,2},{4,5},{5,4},{6,7},{7,6},{8,9},{9,8},{10,11... | collective-permute-start | bytes 1277960 | tf_op jit(solution)/shard_map/ppermute | solution.py:87
  58.8 35.3 %collective-permute-start.5 = (bf16[32,2048]{1,0:T(8,128)(2,1)}, bf16[32,2048]{1,0:T(8,128)(2,1)S(1)}, u32[]{:S(2)}, u32[]{:S(2)}) collective-permute-start(bf16[32,2048]{1,0:T(8,128)(2,1)} %get-tuple-element.73), channel_id=1, source_target_pairs={{0,6},{1,7},{2,0},{3,1},{4,2},{5,3},{6,4},{7,5},{8,14},{9,15},{10,... | collective-permute-start | bytes 393224 | tf_op jit(solution)/shard_map/ppermute | solution.py:87
  58.8 35.3 %collective-permute-start.4 = (bf16[32,2048]{1,0:T(8,128)(2,1)}, bf16[32,2048]{1,0:T(8,128)(2,1)S(1)}, u32[]{:S(2)}, u32[]{:S(2)}) collective-permute-start(bf16[32,2048]{1,0:T(8,128)(2,1)} %get-tuple-element.73), channel_id=1, source_target_pairs={{0,4},{1,5},{2,6},{3,7},{4,0},{5,1},{6,2},{7,3},{8,12},{9,13},{10,... | collective-permute-start | bytes 393224 | tf_op jit(solution)/shard_map/ppermute | solution.py:87
  61.9 33.6 %collective-permute-start.3 = (bf16[32,2048]{1,0:T(8,128)(2,1)}, bf16[32,2048]{1,0:T(8,128)(2,1)}, u32[]{:S(2)}, u32[]{:S(2)}) collective-permute-start(bf16[32,2048]{1,0:T(8,128)(2,1)} %get-tuple-element.73), channel_id=1, source_target_pairs={{0,2},{1,3},{2,4},{3,5},{4,6},{5,7},{6,0},{7,1},{8,10},{9,11},{10,... | collective-permute-start | bytes 393224 | tf_op jit(solution)/shard_map/ppermute | solution.py:87
  63.9 0.8 copy-start.8
  94.2 8.0 %copy-start.4 = (bf16[128,1536]{1,0:T(8,128)(2,1)S(1)}, bf16[128,1536]{1,0:T(8,128)(2,1)}, u32[]{:S(2)}) copy-start(bf16[128,1536]{1,0:T(8,128)(2,1)} %get-tuple-element.84.refs_0_.refs_4_) | copy-start | bytes 1179652
  94.2 0.7 copy-start.11
  94.8 0.6 copy-start.12
  95.5 9.4 %copy-start = (bf16[4,96,1536]{2,1,0:T(8,128)(2,1)}, bf16[4,96,1536]{2,1,0:T(8,128)(2,1)S(1)}, u32[]{:S(2)}) copy-start(bf16[4,96,1536]{2,1,0:T(8,128)(2,1)S(1)} %all-to-all-done.1.refs_2_.refs_6_) | copy-start | bytes 3538948
  95.5 9.4 %collective-permute-start.12 = (bf16[4,96,1536]{2,1,0:T(8,128)(2,1)S(1)}, bf16[4,96,1536]{2,1,0:T(8,128)(2,1)}, u32[]{:S(2)}, u32[]{:S(2)}) collective-permute-start(bf16[4,96,1536]{2,1,0:T(8,128)(2,1)S(1)} %all-to-all-done.1.refs_2_.refs_6_), channel_id=1, source_target_pairs={{0,1},{1,0},{2,3},{3,2},{4,5},{5,4},{6,7},{7,6},{8,9},{9,8},{10,11... | collective-permute-start | bytes 3538952 | tf_op jit(solution)/shard_map/ppermute | solution.py:87
  98.3 34.6 %all-to-all-start.2 = ((bf16[4,96,2048]{2,1,0:T(8,128)(2,1)}), bf16[4,96,2048]{2,1,0:T(8,128)(2,1)S(1)}, u32[]{:S(2)}, u32[]{:S(2)}) async-start(bf16[4,96,2048]{2,1,0:T(8,128)(2,1)} %broadcast_in_dim.10), calls=%async_computation.2 | async-start | bytes 3145728 | tf_op jit(solution)/shard_map/all_to_all | solution.py:95
  102.1 99.5 %all-gather.3.cloned.1.call-start = ((), (), s32[]{:S(2)}) async-start(), calls=%async_computation.4 | async-start | bytes 4718592 | tf_op jit(solution)/shard_map/all_gather | solution.py:711
  102.1 2.8 collective-permute-start.11
  102.2 29.4 %collective-permute-start.10 = (bf16[32,2048]{1,0:T(8,128)(2,1)}, bf16[32,2048]{1,0:T(8,128)(2,1)S(1)}, u32[]{:S(2)}, u32[]{:S(2)}) collective-permute-start(bf16[32,2048]{1,0:T(8,128)(2,1)} %get-tuple-element.83), channel_id=1, source_target_pairs={{0,6},{1,7},{2,0},{3,1},{4,2},{5,3},{6,4},{7,5},{8,14},{9,15},{10,... | collective-permute-start | bytes 393224 | tf_op jit(solution)/shard_map/ppermute | solution.py:87
  104.0 27.6 %collective-permute-start.9 = (bf16[32,2048]{1,0:T(8,128)(2,1)}, bf16[32,2048]{1,0:T(8,128)(2,1)S(1)}, u32[]{:S(2)}, u32[]{:S(2)}) collective-permute-start(bf16[32,2048]{1,0:T(8,128)(2,1)} %get-tuple-element.83), channel_id=1, source_target_pairs={{0,4},{1,5},{2,6},{3,7},{4,0},{5,1},{6,2},{7,3},{8,12},{9,13},{10,... | collective-permute-start | bytes 393224 | tf_op jit(solution)/shard_map/ppermute | solution.py:87
  104.0 28.9 %collective-permute-start.8 = (bf16[32,2048]{1,0:T(8,128)(2,1)}, bf16[32,2048]{1,0:T(8,128)(2,1)}, u32[]{:S(2)}, u32[]{:S(2)}) collective-permute-start(bf16[32,2048]{1,0:T(8,128)(2,1)} %get-tuple-element.83), channel_id=1, source_target_pairs={{0,2},{1,3},{2,4},{3,5},{4,6},{5,7},{6,0},{7,1},{8,10},{9,11},{10,... | collective-permute-start | bytes 393224 | tf_op jit(solution)/shard_map/ppermute | solution.py:87
  104.9 0.7 copy-start.5
  131.6 0.7 copy-start.9
  132.3 0.7 copy-start.10
  132.9 9.4 %copy-start.2 = (bf16[4,96,2048]{2,1,0:T(8,128)(2,1)}, bf16[4,96,2048]{2,1,0:T(8,128)(2,1)S(1)}, u32[]{:S(2)}) copy-start(bf16[4,96,2048]{2,1,0:T(8,128)(2,1)S(1)} %all-to-all-done.2.refs_3_) | copy-start | bytes 4718596
  133.0 9.4 %collective-permute-start.15 = (bf16[4,96,2048]{2,1,0:T(8,128)(2,1)S(1)}, bf16[4,96,2048]{2,1,0:T(8,128)(2,1)}, u32[]{:S(2)}, u32[]{:S(2)}) collective-permute-start(bf16[4,96,2048]{2,1,0:T(8,128)(2,1)S(1)} %all-to-all-done.2.refs_3_), channel_id=1, source_target_pairs={{0,1},{1,0},{2,3},{3,2},{4,5},{5,4},{6,7},{7,6},{8,9},{9,8},{10,11... | collective-permute-start | bytes 4718600 | tf_op jit(solution)/shard_map/ppermute | solution.py:87
  135.9 61.1 %all-to-all-start.3 = ((bf16[4,96,2048]{2,1,0:T(8,128)(2,1)}), bf16[4,96,2048]{2,1,0:T(8,128)(2,1)S(1)}, u32[]{:S(2)}, u32[]{:S(2)}) async-start(bf16[4,96,2048]{2,1,0:T(8,128)(2,1)} %broadcast_in_dim.11), calls=%async_computation.3 | async-start | bytes 3145728 | tf_op jit(solution)/shard_map/all_to_all | solution.py:95
  140.1 2.3 collective-permute-start.14
  197.0 4.6 %copy-start.1 = (bf16[4,96,2048]{2,1,0:T(8,128)(2,1)}, bf16[4,96,2048]{2,1,0:T(8,128)(2,1)S(1)}, u32[]{:S(2)}) copy-start(bf16[4,96,2048]{2,1,0:T(8,128)(2,1)S(1)} %all-to-all-done.3.refs_3_) | copy-start | bytes 4718596
  197.0 4.6 %collective-permute-start.16 = (bf16[4,96,2048]{2,1,0:T(8,128)(2,1)S(1)}, bf16[4,96,2048]{2,1,0:T(8,128)(2,1)S(1)}, u32[]{:S(2)}, u32[]{:S(2)}) collective-permute-start(bf16[4,96,2048]{2,1,0:T(8,128)(2,1)S(1)} %all-to-all-done.3.refs_3_), channel_id=1, source_target_pairs={{0,1},{1,0},{2,3},{3,2},{4,5},{5,4},{6,7},{7,6},{8,9},{9,8},{10,11... | collective-permute-start | bytes 4718600 | tf_op jit(solution)/shard_map/ppermute | solution.py:87
  197.3 4.3 %collective-permute-start.13 = (bf16[128,2048]{1,0:T(8,128)(2,1)}, bf16[128,2048]{1,0:T(8,128)(2,1)}, u32[]{:S(2)}, u32[]{:S(2)}) collective-permute-start(bf16[128,2048]{1,0:T(8,128)(2,1)} %get-tuple-element.98.refs_1_), channel_id=1, source_target_pairs={{0,1},{1,0},{2,3},{3,2},{4,5},{5,4},{6,7},{7,6},{8,9},{9,8},{10,11... | collective-permute-start | bytes 1572872 | tf_op jit(solution)/shard_map/ppermute | solution.py:87
  201.6 1.2 copy-start.6
  306.5 1.5 collective-permute-start.17
  308.9 5.4 %collective-permute-start.20 = (f32[16,1024]{1,0:T(8,128)S(1)}, f32[16,1024]{1,0:T(8,128)S(1)}, u32[]{:S(2)}, u32[]{:S(2)}) collective-permute-start(f32[16,1024]{1,0:T(8,128)S(1)} %add.21), channel_id=1, source_target_pairs={{0,24},{1,25},{2,26},{3,27},{4,28},{5,29},{6,30},{7,31},{8,16},{9,... | collective-permute-start | bytes 196616 | tf_op jit(solution)/shard_map/ppermute | solution.py:87
  311.8 4.3 %collective-permute-start.19 = (f32[16,1024]{1,0:T(8,128)S(1)}, f32[16,1024]{1,0:T(8,128)S(1)}, u32[]{:S(2)}, u32[]{:S(2)}) collective-permute-start(f32[16,1024]{1,0:T(8,128)S(1)} %add.21), channel_id=1, source_target_pairs={{0,16},{1,17},{2,18},{3,19},{4,20},{5,21},{6,22},{7,23},{8,24},{9,... | collective-permute-start | bytes 196616 | tf_op jit(solution)/shard_map/ppermute | solution.py:87
  312.3 4.3 %collective-permute-start.18 = (f32[16,1024]{1,0:T(8,128)S(1)}, f32[16,1024]{1,0:T(8,128)S(1)}, u32[]{:S(2)}, u32[]{:S(2)}) collective-permute-start(f32[16,1024]{1,0:T(8,128)S(1)} %add.21), channel_id=1, source_target_pairs={{0,8},{1,9},{2,10},{3,11},{4,12},{5,13},{6,14},{7,15},{8,0},{9,1},... | collective-permute-start | bytes 196616 | tf_op jit(solution)/shard_map/ppermute | solution.py:87
  316.6 31.5 %collective-permute-start.23 = (f32[16,1024]{1,0:T(8,128)S(1)}, f32[16,1024]{1,0:T(8,128)S(1)}, u32[]{:S(2)}, u32[]{:S(2)}) collective-permute-start(f32[16,1024]{1,0:T(8,128)S(1)} %add_add_fusion.1), channel_id=1, source_target_pairs={{0,6},{1,7},{2,0},{3,1},{4,2},{5,3},{6,4},{7,5},{8,14},{9,15},{10,... | collective-permute-start | bytes 196616 | tf_op jit(solution)/shard_map/ppermute | solution.py:87
  319.7 28.4 %collective-permute-start.22 = (f32[16,1024]{1,0:T(8,128)S(1)}, f32[16,1024]{1,0:T(8,128)S(1)}, u32[]{:S(2)}, u32[]{:S(2)}) collective-permute-start(f32[16,1024]{1,0:T(8,128)S(1)} %add_add_fusion.1), channel_id=1, source_target_pairs={{0,4},{1,5},{2,6},{3,7},{4,0},{5,1},{6,2},{7,3},{8,12},{9,13},{10,... | collective-permute-start | bytes 196616 | tf_op jit(solution)/shard_map/ppermute | solution.py:87
  320.8 27.2 %collective-permute-start.21 = (f32[16,1024]{1,0:T(8,128)S(1)}, f32[16,1024]{1,0:T(8,128)S(1)}, u32[]{:S(2)}, u32[]{:S(2)}) collective-permute-start(f32[16,1024]{1,0:T(8,128)S(1)} %add_add_fusion.1), channel_id=1, source_target_pairs={{0,2},{1,3},{2,4},{3,5},{4,6},{5,7},{6,0},{7,1},{8,10},{9,11},{10,... | collective-permute-start | bytes 196616 | tf_op jit(solution)/shard_map/ppermute | solution.py:87
Sparse Core Ops, SparseCore 0:
  33.4 85.0 all-gather.4
  133.1 48.3 all-gather.2
